TPU v7x, 32 devices: a whole 2x2x4 slice. The times are simulated.
32 devices in a mesh: dp: 4 (over x, core), wide: 8 (over z, y).
Axes of the slice: x: 2, y: 2, z: 4, core: 2. Of those that a mesh axis runs over, the one named last changes fastest.
Arguments:
- inputs: bfloat16 [32, 256, 2048], P(('dp', 'wide')), may hold values from -6 to 6
- cotangent: bfloat16 [32, 256, 2048], P(('dp', 'wide')), may hold values from -6 to 6
- keep_mask: int32 [32], P(('dp', 'wide')), may hold values 0 or 1
- positions: int32 [32, 256], P(('dp', 'wide')), may hold values from 0 to 510, as said below
- master_weights: float32 [172, 262144], P(None, ('dp', 'wide'))
- gains: float32 [2, 2048], replicated, may hold values from 0.5 to 1.5
- gain_moments: float32 [2, 2048], replicated, may hold values from 40.96 to 163.84
- block_slot: int32 [172], replicated, may hold values from 0 to 191, as said below
- stat_left: float32 [192, 512, 512], P(('dp', 'wide')), as said below
- stat_right: float32 [192, 512, 512], P(('dp', 'wide')), as said below
- root_left: float32 [192, 512, 512], P(('dp', 'wide')), as said below
- root_right: float32 [192, 512, 512], P(('dp', 'wide')), as said below
Outputs:
- output: bfloat16 [32, 256, 2048], P(('dp', 'wide'))
- input_grad: bfloat16 [32, 256, 2048], P(('dp', 'wide'))
- weight_grads: float32 [172, 262144], P(None, ('dp', 'wide'))
- new_left: float32 [192, 512, 512], P(('dp', 'wide'))
- new_right: float32 [192, 512, 512], P(('dp', 'wide'))
- new_weights: float32 [172, 262144], P(None, ('dp', 'wide'))
- gain_grads: float32 [2, 2048], replicated
- new_gain_moments: float32 [2, 2048], replicated
- new_gains: float32 [2, 2048], replicated
Inputs may be any that keep to these rules, and one draw needn't show every extreme that they name: `block_slot`: distinct slots, one for each block; slots 0 and 191 always own a block. Each sequence's positions start at 0, rise by at least 1 from one token to the next (mostly by 1 or 2), and its last token is at 510. `stat_left`: symmetric positive definite. `stat_right`: symmetric positive definite. `root_left`: symmetric. `root_right`: symmetric.
All inputs are finite; a program needn't handle non-finite values. No bound on the sum of `keep_mask` on one device may be relied on, other than what follows from the above.
Results may differ from a plain program's by a relative error of at most 0.017.
Values may be sent and summed in bfloat16 or wider, within the bound.
A program may use at most 512 MiB of HBM per device.

v0:
```python
import jax
import jax.numpy as jnp
from jax import lax
from jax.sharding import PartitionSpec as P

D = 2048
HEADS = 16
HD = 128
KVH = 4
FF = 5632
B = 512
SEQ = 256
LAYER = 16
DEPTH = 24
STEP = 10
RAMP = 20
NBLK = 172


norm_eps = 1e-05
stat_decay = 0.95
weight_rate = 0.5
weight_decay = 0.001
gain_rate = 0.05
adam_eps = 1e-08
rope_base = 10000.0
scale_eps = 1e-06
masked_value = -1e30


def keep_rate():
    return 1.0 - 0.2 * (2.0 ** (LAYER / (DEPTH - 1)) - 1.0) * min(STEP / RAMP, 1.0)


def block_shapes():
    rows_model = D // B
    rows_kv = KVH * HD // B
    rows_ff = FF // B
    return [
        (rows_model, rows_model),
        (rows_model, rows_kv),
        (rows_model, rows_kv),
        (rows_model, rows_model),
        (rows_model, rows_ff),
        (rows_model, rows_ff),
        (rows_ff, rows_model),
    ]


def block_scale(block_index):
    bounds = []
    running = 0
    for row_blocks, col_blocks in block_shapes():
        running = running + row_blocks * col_blocks
        bounds.append(running)
    plain_scale = D ** (-0.5)
    out_scale = (SEQ / 8.0) ** 0.5 * D ** (-0.5)
    return jnp.where(
        block_index < bounds[2],
        plain_scale,
        jnp.where(
            block_index < bounds[3],
            out_scale,
            jnp.where(block_index < bounds[5], plain_scale, FF ** (-0.5)),
        ),
    ).astype(jnp.float32)


def rope_tables(position):
    half_dim = HD // 2
    freqs = rope_base ** (-(jnp.arange(half_dim).astype(jnp.float32) * 2.0 / HD))
    angles = position.astype(jnp.float32)[:, None] * freqs[None, :]
    cosine_table = jnp.concatenate([jnp.cos(angles), jnp.cos(angles)], -1)
    sine_table = jnp.concatenate([jnp.sin(angles), jnp.sin(angles)], -1)
    return (cosine_table, sine_table)


def rotate(values, cosine_table, sine_table):
    half_dim = HD // 2
    turned = jnp.concatenate([-values[..., half_dim:], values[..., :half_dim]], -1)
    return values * cosine_table[:, None, :] + turned * sine_table[:, None, :]


def split_blocks(whole, shapes):
    matrices = []
    first_row = 0
    for row_blocks, col_blocks in shapes:
        row_count = row_blocks * col_blocks
        blocks = whole[first_row : first_row + row_count].reshape(row_blocks, col_blocks, B, B)
        matrices.append(blocks.transpose(0, 2, 1, 3).reshape(row_blocks * B, col_blocks * B))
        first_row = first_row + row_count
    return matrices


def apply_blocks(rows, matrix):
    return jnp.dot(rows, matrix, preferred_element_type=jnp.float32)


def apply_back(grads, matrix):
    return lax.dot_general(
        grads, matrix, (((1,), (1,)), ((), ())), preferred_element_type=jnp.float32
    )


def block_grad(rows, grads, row_blocks, col_blocks):
    dense = lax.dot_general(
        rows, grads, (((0,), (0,)), ((), ())), preferred_element_type=jnp.float32
    )
    return (
        dense.reshape(row_blocks, B, col_blocks, B)
        .transpose(0, 2, 1, 3)
        .reshape(row_blocks * col_blocks, B * B)
    )


def norm_forward(values, gain):
    rate = lax.rsqrt(jnp.mean(values * values, -1, keepdims=True) + norm_eps)
    return (values * rate * gain, rate)


def norm_backward(values, rate, gain, grads):
    scaled = grads * gain
    value_grad = rate * scaled - values * rate * rate * rate * jnp.mean(
        values * scaled, -1, keepdims=True
    )
    gain_grad = jnp.sum(grads * values * rate, 0)
    return (value_grad, gain_grad)


def attention_scores(query_rows, key_rows):
    seq_len = query_rows.shape[0]
    grouped = query_rows.reshape(seq_len, KVH, HEADS // KVH, HD)
    scores = jnp.einsum(
        "skgd,tkd->kgst", grouped, key_rows, preferred_element_type=jnp.float32
    ) * HD ** (-0.5)
    causal = jnp.arange(seq_len)[:, None] >= jnp.arange(seq_len)[None, :]
    return jnp.where(causal, scores, masked_value)


def local(
    inputs,
    cotangent,
    keep_mask,
    positions,
    master_weights,
    gains,
    gain_moments,
    block_slot,
    stat_left,
    stat_right,
    root_left,
    root_right,
):
    shapes = block_shapes()
    n_attn = sum([row_blocks * col_blocks for row_blocks, col_blocks in shapes[:4]])
    rows_model, rows_kv = shapes[1]
    rows_ff = shapes[6][0]
    seq_len = inputs.shape[1]
    group_size = HEADS // KVH
    score_scale = HD ** (-0.5)
    slot_dev = stat_left.shape[0]
    slots_all = slot_dev * lax.axis_size(("dp", "wide"))
    piece_len = master_weights.shape[1]
    residual = inputs[0].astype(jnp.float32)
    branch_scale = keep_mask[0].astype(jnp.float32) / keep_rate()
    cosine_table, sine_table = rope_tables(positions[0])
    attn_whole = lax.all_gather(
        master_weights[:n_attn].astype(jnp.bfloat16), ("dp", "wide"), axis=1, tiled=True
    )
    w_query, w_key, w_value, w_out = split_blocks(attn_whole, shapes[:4])
    normed_float, rate_one = norm_forward(residual, gains[0])
    normed_one = normed_float.astype(jnp.bfloat16)
    query_rows = rotate(
        apply_blocks(normed_one, w_query).reshape(seq_len, HEADS, HD), cosine_table, sine_table
    ).astype(jnp.bfloat16)
    key_rows = rotate(
        apply_blocks(normed_one, w_key).reshape(seq_len, KVH, HD), cosine_table, sine_table
    ).astype(jnp.bfloat16)
    value_rows = apply_blocks(normed_one, w_value).astype(jnp.bfloat16).reshape(seq_len, KVH, HD)
    scores = attention_scores(query_rows, key_rows)
    row_top = jnp.max(scores, -1, keepdims=True)
    exp_scores = jnp.exp(scores - row_top)
    row_total = jnp.sum(exp_scores, -1, keepdims=True)
    log_total = row_top + jnp.log(row_total)
    probs_low = (exp_scores / row_total).astype(jnp.bfloat16)
    attn_out = jnp.einsum(
        "kgst,tkd->skgd", probs_low, value_rows, preferred_element_type=jnp.float32
    )
    out_low = attn_out.reshape(seq_len, D).astype(jnp.bfloat16)
    middle = residual + branch_scale * apply_blocks(out_low, w_out)
    mlp_whole = lax.all_gather(
        master_weights[n_attn:].astype(jnp.bfloat16), ("dp", "wide"), axis=1, tiled=True
    )
    w_gate, w_up, w_down = split_blocks(mlp_whole, shapes[4:])
    normed_float, rate_two = norm_forward(middle, gains[1])
    normed_two = normed_float.astype(jnp.bfloat16)
    gate_rows = apply_blocks(normed_two, w_gate)
    up_rows = apply_blocks(normed_two, w_up)
    sigmoid_gate = jax.nn.sigmoid(gate_rows)
    hidden = (gate_rows * sigmoid_gate * up_rows).astype(jnp.bfloat16)
    result = middle + branch_scale * apply_blocks(hidden, w_down)
    output = result.astype(jnp.bfloat16)[None]
    out_grad_f = cotangent[0].astype(jnp.float32)
    down_low = (branch_scale * out_grad_f).astype(jnp.bfloat16)
    back_gate, back_up, back_down = (w_gate, w_up, w_down)
    grad_down = block_grad(hidden, down_low, rows_ff, rows_model)
    hidden_grad = apply_back(down_low, back_down)
    gate_low = (
        hidden_grad * up_rows * sigmoid_gate * (1.0 + gate_rows * (1.0 - sigmoid_gate))
    ).astype(jnp.bfloat16)
    up_low = (hidden_grad * gate_rows * sigmoid_gate).astype(jnp.bfloat16)
    grad_gate = block_grad(normed_two, gate_low, rows_model, rows_ff)
    grad_up = block_grad(normed_two, up_low, rows_model, rows_ff)
    mlp_pieces = (
        lax.psum_scatter(grad_gate, ("dp", "wide"), scatter_dimension=1, tiled=True),
        lax.psum_scatter(grad_up, ("dp", "wide"), scatter_dimension=1, tiled=True),
        lax.psum_scatter(grad_down, ("dp", "wide"), scatter_dimension=1, tiled=True),
    )
    normed_two_grad = apply_back(gate_low, back_gate) + apply_back(up_low, back_up)
    middle_local, gain_two = norm_backward(middle, rate_two, gains[1], normed_two_grad)
    middle_grad = out_grad_f + middle_local
    proj_low = (branch_scale * middle_grad).astype(jnp.bfloat16)
    back_query, back_key, back_value, back_out = (w_query, w_key, w_value, w_out)
    grad_out = block_grad(out_low, proj_low, rows_model, rows_model)
    attn_grad_low = apply_back(proj_low, back_out).astype(jnp.bfloat16)
    scores = attention_scores(query_rows, key_rows)
    probs_float = jnp.exp(scores - log_total)
    probs_low = probs_float.astype(jnp.bfloat16)
    grad_grouped = attn_grad_low.reshape(seq_len, KVH, group_size, HD)
    query_grouped = query_rows.reshape(seq_len, KVH, group_size, HD)
    prob_grads = jnp.einsum(
        "skgd,tkd->kgst", grad_grouped, value_rows, preferred_element_type=jnp.float32
    )
    row_dot = jnp.sum(prob_grads * probs_float, -1, keepdims=True)
    score_low = (probs_float * (prob_grads - row_dot)).astype(jnp.bfloat16)
    query_grad = (
        jnp.einsum("kgst,tkd->skgd", score_low, key_rows, preferred_element_type=jnp.float32)
        * score_scale
    )
    key_grad = (
        jnp.einsum("kgst,skgd->tkd", score_low, query_grouped, preferred_element_type=jnp.float32)
        * score_scale
    )
    value_grad = jnp.einsum(
        "kgst,skgd->tkd", probs_low, grad_grouped, preferred_element_type=jnp.float32
    )
    query_low = (
        rotate(query_grad.reshape(seq_len, HEADS, HD), cosine_table, -sine_table)
        .reshape(seq_len, D)
        .astype(jnp.bfloat16)
    )
    key_low = (
        rotate(key_grad, cosine_table, -sine_table).reshape(seq_len, KVH * HD).astype(jnp.bfloat16)
    )
    value_low = value_grad.reshape(seq_len, KVH * HD).astype(jnp.bfloat16)
    grad_query = block_grad(normed_one, query_low, rows_model, rows_model)
    grad_key = block_grad(normed_one, key_low, rows_model, rows_kv)
    grad_value = block_grad(normed_one, value_low, rows_model, rows_kv)
    normed_one_grad = (
        apply_back(query_low, back_query)
        + apply_back(key_low, back_key)
        + apply_back(value_low, back_value)
    )
    input_local, gain_one = norm_backward(residual, rate_one, gains[0], normed_one_grad)
    input_grad = (middle_grad + input_local).astype(jnp.bfloat16)[None]
    gain_grads = lax.psum(jnp.stack([gain_one, gain_two]), ("dp", "wide"))
    new_gain_moments = stat_decay * gain_moments + (1.0 - stat_decay) * gain_grads * gain_grads
    new_gains = gains - gain_rate * gain_grads / (jnp.sqrt(new_gain_moments) + adam_eps)
    slot_block = jnp.full((slots_all,), -1, jnp.int32).at[block_slot].set(jnp.arange(NBLK))
    attn_pieces = (
        lax.psum_scatter(grad_query, ("dp", "wide"), scatter_dimension=1, tiled=True),
        lax.psum_scatter(grad_key, ("dp", "wide"), scatter_dimension=1, tiled=True),
        lax.psum_scatter(grad_value, ("dp", "wide"), scatter_dimension=1, tiled=True),
        lax.psum_scatter(grad_out, ("dp", "wide"), scatter_dimension=1, tiled=True),
    )
    grad_local = jnp.concatenate(list(attn_pieces) + list(mlp_pieces), 0)
    send_rows = jnp.zeros((slots_all, piece_len), jnp.float32).at[block_slot].set(grad_local)
    owned_grads = lax.all_to_all(
        send_rows.astype(jnp.bfloat16), ("dp", "wide"), split_axis=0, concat_axis=1, tiled=True
    ).astype(send_rows.dtype)
    grad_blocks = owned_grads.reshape(slot_dev, B, B)
    new_left = stat_decay * stat_left + (1.0 - stat_decay) * jnp.einsum(
        "nij,nkj->nik", grad_blocks, grad_blocks, precision=lax.Precision.HIGHEST
    )
    new_right = stat_decay * stat_right + (1.0 - stat_decay) * jnp.einsum(
        "nji,njk->nik", grad_blocks, grad_blocks, precision=lax.Precision.HIGHEST
    )
    precond = jnp.einsum("nij,njk->nik", root_left, grad_blocks, precision=lax.Precision.HIGHEST)
    precond = jnp.einsum("nij,njk->nik", precond, root_right, precision=lax.Precision.HIGHEST)
    own_blocks = lax.dynamic_slice_in_dim(
        slot_block, lax.axis_index(("dp", "wide")) * slot_dev, slot_dev
    )
    own_scale = jnp.where(own_blocks >= 0, block_scale(jnp.maximum(own_blocks, 0)), 0.0)
    steps_local = (
        weight_rate
        * own_scale[:, None, None]
        * precond
        * lax.rsqrt(jnp.mean(precond * precond, axis=(1, 2), keepdims=True) + scale_eps)
    )
    steps_local = steps_local.reshape(slot_dev, B * B)
    returned_steps = lax.all_to_all(
        steps_local.astype(jnp.bfloat16), ("dp", "wide"), split_axis=1, concat_axis=0, tiled=True
    ).astype(steps_local.dtype)
    new_weights = (1.0 - weight_decay) * master_weights - returned_steps[block_slot]
    return (
        output,
        input_grad,
        grad_local,
        new_left,
        new_right,
        new_weights,
        gain_grads,
        new_gain_moments,
        new_gains,
    )


def solution(mesh):
    placed = (
        P(("dp", "wide"), None, None),
        P(("dp", "wide"), None, None),
        P(("dp", "wide")),
        P(("dp", "wide"), None),
        P(None, ("dp", "wide")),
        P(),
        P(),
        P(),
        P(("dp", "wide"), None, None),
        P(("dp", "wide"), None, None),
        P(("dp", "wide"), None, None),
        P(("dp", "wide"), None, None),
    )
    return jax.shard_map(
        local,
        mesh=mesh,
        in_specs=placed,
        out_specs=(
            P(("dp", "wide"), None, None),
            P(("dp", "wide"), None, None),
            P(None, ("dp", "wide")),
            P(("dp", "wide"), None, None),
            P(("dp", "wide"), None, None),
            P(None, ("dp", "wide")),
            P(),
            P(),
            P(),
        ),
        check_vma=False,
    )
```

profile of v0, /device:TPU:0, one launch (start us, length us, event | category | flops | bytes accessed | tf_op | source)
XLA Modules:
  0.0 3543.6 jit_solution(9709322681676140687)
XLA Ops:
  18.3 131.9 %all-gather.3.cloned.1.call-done = bf16[40,262144]{1,0:T(8,128)(2,1)} async-done(((bf16[40,8192]{1,0:T(8,128)(2,1)}), bf16[40,262144]{1,0:T(8,128)(2,1)}) %all-gather.3.cloned.1.call-update) | async-done | bytes 20971536 | tf_op jit(solution)/shard_map/all_gather | solution.py:167
  150.1 12.2 fusion.96
  162.4 10.5 copy.159
  172.8 12.2 copy.101
  185.0 10.3 copy.160
  195.3 9.8 copy.157
  205.1 15.4 copy.96
  220.5 10.7 copy.158
  231.2 6.2 fusion.97
  252.9 6.1 fusion.62
  271.1 257.1 %all-gather.5.cloned.1.call-done = bf16[132,262144]{1,0:T(8,128)(2,1)} async-done(((bf16[132,8192]{1,0:T(8,128)(2,1)}), bf16[132,262144]{1,0:T(8,128)(2,1)}) %all-gather.5.cloned.1.call-update) | async-done | bytes 69206032 | tf_op jit(solution)/shard_map/all_gather | solution.py:191
  528.1 41.8 %fusion.95 = (bf16[44,262144]{1,0:T(8,128)(2,1)S(1)}, bf16[44,262144]{1,0:T(8,128)(2,1)}, bf16[44,262144]{1,0:T(8,128)(2,1)}) fusion(bf16[132,262144]{1,0:T(8,128)(2,1)} %all-gather.5.cloned.1.call-done), kind=kLoop, calls=%fused_computation.158 | loop fusion | bytes 138412032 | tf_op jit(solution)/shard_map/slice | solution.py:89
  569.9 17.1 copy.161
  587.0 19.8 slice.99
  606.8 38.7 %copy.102 = bf16[4,11,512,512]{2,0,3,1:T(4,128)(2,1)} copy(bf16[4,11,512,512]{3,2,1,0:T(8,128)(2,1)} %bitcast.351) | data formatting | bytes 46137344 | tf_op jit(solution)/shard_map/reshape | solution.py:89
  645.6 26.4 copy.162
  672.1 17.4 copy.165
  689.4 19.8 slice.101
  709.3 29.7 copy.104
  739.0 26.4 copy.166
  765.5 17.2 copy.163
  782.7 19.8 slice.100
  802.5 38.8 %copy.103 = bf16[4,11,512,512]{2,0,3,1:T(4,128)(2,1)} copy(bf16[4,11,512,512]{3,2,1,0:T(8,128)(2,1)} %bitcast.355) | data formatting | bytes 46137344 | tf_op jit(solution)/shard_map/reshape | solution.py:89
  841.3 23.9 copy.164
  865.2 13.3 fusion.100
  878.5 15.1 fusion
  893.6 14.4 multiply_convert_fusion.1
  908.0 14.3 fusion.101
  922.3 12.7 multiply_reduce_fusion.1
  952.8 7.0 reshape_transpose_reshape.15
  964.7 7.1 reshape_transpose_reshape.14
  989.4 22.6 copy.167
  1016.3 22.6 copy.168
  1044.6 19.3 fusion.107
  1064.0 35.0 pad.17
  1099.0 46.9 %copy.171 = f32[6,8,512,512]{3,1,2,0:T(8,128)} copy(f32[6,8,512,512]{3,2,1,0:T(8,128)} %bitcast.334) | data formatting | bytes 100663296
  1147.1 20.3 fusion.106
  1167.4 54.2 %reshape.318 = f32[4,512,11,512]{1,0,3,2:T(4,128)} reshape(f32[2048,5632]{0,1:T(8,128)} %fusion.106) | data formatting | bytes 92274688 | tf_op jit(solution)/shard_map/reshape | solution.py:110
  1221.6 52.0 %copy.116 = f32[4,11,512,512]{3,2,1,0:T(8,128)} copy(f32[4,11,512,512]{2,0,3,1:T(4,128)} %bitcast.337) | data formatting | bytes 92274688 | tf_op jit(solution)/shard_map/transpose | solution.py:111
  1273.6 34.7 pad.16
  1308.3 45.9 %copy.170 = f32[6,8,512,512]{3,1,2,0:T(8,128)} copy(f32[6,8,512,512]{3,2,1,0:T(8,128)} %bitcast.335) | data formatting | bytes 100663296
  1354.3 20.4 fusion.105
  1374.7 54.1 %reshape.316 = f32[4,512,11,512]{1,0,3,2:T(4,128)} reshape(f32[2048,5632]{0,1:T(8,128)} %fusion.105) | data formatting | bytes 92274688 | tf_op jit(solution)/shard_map/reshape | solution.py:110
  1428.8 52.0 %copy.114 = f32[4,11,512,512]{3,2,1,0:T(8,128)} copy(f32[4,11,512,512]{2,0,3,1:T(4,128)} %bitcast.338) | data formatting | bytes 92274688 | tf_op jit(solution)/shard_map/transpose | solution.py:111
  1480.9 34.7 pad.15
  1515.6 46.3 %copy.169 = f32[6,8,512,512]{3,1,2,0:T(8,128)} copy(f32[6,8,512,512]{3,2,1,0:T(8,128)} %bitcast.336) | data formatting | bytes 100663296
  1564.4 304.5 %reduce-scatter.10.cloned.1.call-done = f32[16,8192]{1,0:T(8,128)} async-done(((f32[16,262144]{1,0:T(8,128)}), f32[16,8192]{1,0:T(8,128)}) %reduce-scatter.10.cloned.1.call-update) | async-done | bytes 524304 | tf_op jit(solution)/shard_map/reduce_scatter | solution.py:274
  1868.9 435.6 %reduce-scatter.16.cloned.1.call-done = f32[44,8192]{1,0:T(8,128)} async-done(((f32[44,262144]{1,0:T(8,128)}), f32[44,8192]{1,0:T(8,128)}) %reduce-scatter.16.cloned.1.call-update) | async-done | bytes 1441808 | tf_op jit(solution)/shard_map/reduce_scatter | solution.py:217
  2304.5 435.4 %reduce-scatter.14.cloned.1.call-done = f32[44,8192]{1,0:T(8,128)} async-done(((f32[44,262144]{1,0:T(8,128)}), f32[44,8192]{1,0:T(8,128)}) %reduce-scatter.14.cloned.1.call-update) | async-done | bytes 1441808 | tf_op jit(solution)/shard_map/reduce_scatter | solution.py:216
  2739.9 435.4 %reduce-scatter.12.cloned.1.call-done = f32[44,8192]{1,0:T(8,128)} async-done(((f32[44,262144]{1,0:T(8,128)}), f32[44,8192]{1,0:T(8,128)}) %reduce-scatter.12.cloned.1.call-update) | async-done | bytes 1441808 | tf_op jit(solution)/shard_map/reduce_scatter | solution.py:215
  3175.3 21.0 concatenate.34
  3196.4 8.9 scatter_custom_fusion
  3216.3 94.7 %all-to-all-done = bf16[32,6,8192]{2,1,0:T(8,128)(2,1)} async-done(((bf16[32,6,8192]{2,1,0:T(8,128)(2,1)}), bf16[32,6,8192]{2,1,0:T(8,128)(2,1)}, u32[]{:S(2)}, u32[]{:S(2)}) %all-to-all-start) | async-done | bytes 3145760 | tf_op jit(solution)/shard_map/all_to_all | solution.py:278
  3321.0 7.2 fusion.108
  3328.3 13.3 multiply_reduce_fusion
  3344.3 5.9 convert_element_type.210
  3359.7 114.5 %psum.7 = f32[2,2048]{1,0:T(2,128)S(1)} all-reduce(f32[2,2048]{1,0:T(2,128)S(1)} %pad_maximum_fusion.3), channel_id=1, replica_groups=mesh['dp'=4,'wide'=8] {'dp','wide'}, use_global_device_ids=true, to_apply=%region_19.20 | all-reduce | flops 4096 | bytes 32768 | tf_op jit(solution)/shard_map/psum | solution.py:266
  3474.9 15.5 fusion.25
  3490.4 7.7 multiply_add_fusion
  3498.1 7.5 multiply_add_fusion.1
  3505.6 6.2 convert_bitcast_fusion
  3511.8 6.8 reshape.324
  3518.6 9.9 gather_fusion
  3528.6 7.7 multiply_subtract_fusion
  (240 shorter events, 125.3 us)
Async XLA Ops:
  7.2 143.0 %all-gather.3.cloned.1.call-start = ((), (), s32[]{:S(2)}) async-start(), calls=%async_computation.7 | async-start | bytes 21626880 | tf_op jit(solution)/shard_map/all_gather | solution.py:167
  11.8 5.0 copy-start.51
  12.7 5.2 copy-start.2
  12.7 5.5 copy-start.41
  12.7 515.4 %all-gather.5.cloned.1.call-start = ((), (), s32[]{:S(2)}) async-start(), calls=%async_computation.8 | async-start | bytes 73531392 | tf_op jit(solution)/shard_map/all_gather | solution.py:191
  16.1 1546.5 %all-reduce.5.cloned.1.call-start = ((), (), s32[]{:S(2)}) async-start(), calls=%async_computation.14 | async-start | bytes 16777216
  17.9 241.3 %copy-start.29 = (f32[256,128]{0,1:T(8,128)}, f32[256,128]{0,1:T(8,128)S(1)}, u32[]{:S(2)}) copy-start(f32[256,128]{0,1:T(8,128)S(1)} %get-tuple-element.42) | copy-start | bytes 393220
  18.2 234.7 %copy-start.44 = (f32[256]{0:T(256)}, f32[256]{0:T(256)S(1)}, u32[]{:S(2)}) copy-start(f32[256]{0:T(256)S(1)} %add_rsqrt_fusion.1) | copy-start | bytes 3076
  18.2 234.7 %copy-start.36 = (f32[1,2048]{1,0:T(1,128)}, f32[1,2048]{1,0:T(1,128)S(1)}, u32[]{:S(2)}) copy-start(f32[1,2048]{1,0:T(1,128)S(1)} %get-tuple-element.46) | copy-start | bytes 24580
  18.3 250.9 %copy-start.39 = (f32[1,2048]{1,0:T(1,128)}, f32[1,2048]{1,0:T(1,128)S(1)}, u32[]{:S(2)}) copy-start(f32[1,2048]{1,0:T(1,128)S(1)} %get-tuple-element.45) | copy-start | bytes 24580
  240.8 3.2 copy-start.15
  247.5 5.2 copy-start.4
  252.9 6.8 copy-start.22
  260.5 2.1 copy-start
  260.6 4.1 slice-start.14
  261.2 4.7 slice-start.15
  262.7 5.8 copy-start.17
  268.5 2.6 copy-start.48
  645.5 26.5 slice-start.6
  645.5 26.5 slice-start.7
  645.5 26.5 slice-start.8
  645.5 26.5 slice-start.9
  645.5 26.5 slice-start.10
  645.6 26.5 slice-start.11
  739.0 26.5 slice-start
  739.0 26.5 slice-start.1
  739.0 26.5 slice-start.2
  739.0 26.5 slice-start.3
  739.0 26.5 slice-start.4
  739.0 26.5 slice-start.5
  841.3 23.9 copy-start.8
  878.5 15.1 copy-start.33
  908.0 14.3 copy-start.20
  908.0 14.3 copy-start.21
  908.0 14.3 copy-start.7
  908.0 14.3 copy-start.40
  908.0 14.3 copy-start.49
  908.0 30.7 slice-start.16
  922.3 16.4 slice-start.17
  938.8 3.0 copy-start.38
  941.2 3.8 copy-start.35
  941.7 3.5 copy-start.1
  945.2 4.7 copy-start.26
  947.4 2.4 copy-start.3
  947.4 2.4 copy-start.37
  947.4 2.5 copy-start.45
  952.8 7.1 copy-start.28
  952.8 7.1 copy-start.31
  971.8 592.7 %reduce-scatter.8.cloned.1.call-start = ((), (), s32[]{:S(2)}) async-start(), calls=%async_computation.9 | async-start | bytes 17301504 | tf_op jit(solution)/shard_map/reduce_scatter | solution.py:271
  973.4 2.5 slice-start.12
  974.3 4.0 slice-start.13
  978.3 2.4 copy-start.5
  978.3 2.4 copy-start.25
  1012.0 856.9 %reduce-scatter.10.cloned.1.call-start = ((), (), s32[]{:S(2)}) async-start(), calls=%async_computation.10 | async-start | bytes 17301504 | tf_op jit(solution)/shard_map/reduce_scatter | solution.py:274
  1039.0 1265.6 %reduce-scatter.16.cloned.1.call-start = ((), (), s32[]{:S(2)}) async-start(), calls=%async_computation.13 | async-start | bytes 51904512 | tf_op jit(solution)/shard_map/reduce_scatter | solution.py:217
  1145.9 1594.0 %reduce-scatter.14.cloned.1.call-start = ((), (), s32[]{:S(2)}) async-start(), calls=%async_computation.12 | async-start | bytes 51904512 | tf_op jit(solution)/shard_map/reduce_scatter | solution.py:216
  1354.3 1821.1 %reduce-scatter.12.cloned.1.call-start = ((), (), s32[]{:S(2)}) async-start(), calls=%async_computation.11 | async-start | bytes 51904512 | tf_op jit(solution)/shard_map/reduce_scatter | solution.py:215
  3211.3 99.7 %all-to-all-start = ((bf16[32,6,8192]{2,1,0:T(8,128)(2,1)}), bf16[32,6,8192]{2,1,0:T(8,128)(2,1)}, u32[]{:S(2)}, u32[]{:S(2)}) async-start(bf16[32,6,8192]{2,1,0:T(8,128)(2,1)} %all_to_all.20), calls=%async_computation.5 | async-start | bytes 8388608 | tf_op jit(solution)/shard_map/all_to_all | solution.py:278
  3355.9 3.8 copy-start.46
  3355.9 3.8 copy-start.50
  3355.9 118.3 %copy-start.42 = (f32[2,2048]{1,0:T(2,128)S(1)}, f32[2,2048]{1,0:T(2,128)}, u32[]{:S(2)}) copy-start(f32[2,2048]{1,0:T(2,128)} %param.17) | copy-start | bytes 49156
  3355.9 118.3 %copy-start.47 = (f32[2,2048]{1,0:T(2,128)S(1)}, f32[2,2048]{1,0:T(2,128)}, u32[]{:S(2)}) copy-start(f32[2,2048]{1,0:T(2,128)} %param.18) | copy-start | bytes 49156
  3355.9 149.7 %all-to-all-start.1 = ((bf16[6,32,8192]{2,0,1:T(8,128)(2,1)}), bf16[6,32,8192]{2,0,1:T(8,128)(2,1)}, u32[]{:S(2)}, u32[]{:S(2)}) async-start(bf16[6,32,8192]{2,0,1:T(8,128)(2,1)} %copy.123), calls=%async_computation.6 | async-start | bytes 8388608 | tf_op jit(solution)/shard_map/all_to_all | solution.py:301
  3474.2 16.2 copy-start.43
  (17 other events, 22.1 us)
Sparse Core Ops, SparseCore 0:
  12.8 137.2 all-gather.2
  153.8 374.2 all-gather.4
  971.9 177.1 all-reduce.4
  1151.3 358.1 reduce-scatter.7
  1511.6 357.2 reduce-scatter.9
  1875.2 429.2 reduce-scatter.15
  2311.0 428.9 reduce-scatter.13
  2746.4 428.9 reduce-scatter.11
where the time goes:
time: 3560 us; the launch traced here: 3540 us
  waiting for transfers between devices  2090 us (59%)
  local copies, waits for them, and re-layouts  1050 us (29%)
  matrix products  219 us (6%)
  blocking collectives  115 us (3%)
  other arithmetic  37.2 us (1%)
    unnamed x165, local copies, waits for them, and re-layouts  536 us
    reduce_scatter x1, waiting for transfers between devices, local(): lax.psum_scatter(grad_down, ('dp', 'wide'), scatter_dimension=1, tiled=True)  436 us
    reduce_scatter x1, waiting for transfers between devices, local(): lax.psum_scatter(grad_up, ('dp', 'wide'), scatter_dimension=1, tiled=True)  435 us
    reduce_scatter x1, waiting for transfers between devices, local(): lax.psum_scatter(grad_gate, ('dp', 'wide'), scatter_dimension=1, tiled=True)  435 us
    reduce_scatter x1, waiting for transfers between devices, local(): lax.psum_scatter(grad_out, ('dp', 'wide'), scatter_dimension=1, tiled=True)  304 us
    all_gather x1, waiting for transfers between devices, local(): lax.all_gather(master_weights[n_attn:].astype(jnp.bfloat16), ('dp', 'wide...  257 us
    all_gather x1, waiting for transfers between devices, local(): lax.all_gather(master_weights[:n_attn].astype(jnp.bfloat16), ('dp', 'wide...  132 us
    reshape x4, local copies, waits for them, and re-layouts, split_blocks(): whole[first_row:first_row + row_count].reshape(row_blocks, col_blocks, B, B)  119 us
  transfers between devices with their start and end apart: 10, of which 7 were waited for; matrix products, arithmetic and copies ran while one was open for 21% of the time, Pallas kernels for 0%

commit v1 on v0

v1 whole, which is shorter than its diff:
```python
import functools

import jax
import jax.numpy as jnp
from jax import lax
from jax.experimental import pallas as pl
from jax.experimental.pallas import tpu as pltpu
from jax.sharding import PartitionSpec as P

D = 2048
HEADS = 16
HD = 128
KVH = 4
FF = 5632
B = 512
SEQ = 256
LAYER = 16
DEPTH = 24
STEP = 10
RAMP = 20
NBLK = 172


norm_eps = 1e-05
stat_decay = 0.95
weight_rate = 0.5
weight_decay = 0.001
gain_rate = 0.05
adam_eps = 1e-08
rope_base = 10000.0
scale_eps = 1e-06
masked_value = -1e30


def keep_rate():
    return 1.0 - 0.2 * (2.0 ** (LAYER / (DEPTH - 1)) - 1.0) * min(STEP / RAMP, 1.0)


def block_shapes():
    rows_model = D // B
    rows_kv = KVH * HD // B
    rows_ff = FF // B
    return [
        (rows_model, rows_model),
        (rows_model, rows_kv),
        (rows_model, rows_kv),
        (rows_model, rows_model),
        (rows_model, rows_ff),
        (rows_model, rows_ff),
        (rows_ff, rows_model),
    ]


def block_scale(block_index):
    bounds = []
    running = 0
    for row_blocks, col_blocks in block_shapes():
        running = running + row_blocks * col_blocks
        bounds.append(running)
    plain_scale = D ** (-0.5)
    out_scale = (SEQ / 8.0) ** 0.5 * D ** (-0.5)
    return jnp.where(
        block_index < bounds[2],
        plain_scale,
        jnp.where(
            block_index < bounds[3],
            out_scale,
            jnp.where(block_index < bounds[5], plain_scale, FF ** (-0.5)),
        ),
    ).astype(jnp.float32)


def rope_tables(position):
    half_dim = HD // 2
    freqs = rope_base ** (-(jnp.arange(half_dim).astype(jnp.float32) * 2.0 / HD))
    angles = position.astype(jnp.float32)[:, None] * freqs[None, :]
    cosine_table = jnp.concatenate([jnp.cos(angles), jnp.cos(angles)], -1)
    sine_table = jnp.concatenate([jnp.sin(angles), jnp.sin(angles)], -1)
    return (cosine_table, sine_table)


def rotate(values, cosine_table, sine_table):
    half_dim = HD // 2
    turned = jnp.concatenate([-values[..., half_dim:], values[..., :half_dim]], -1)
    return values * cosine_table[:, None, :] + turned * sine_table[:, None, :]


def norm_rate(values):
    return lax.rsqrt(jnp.mean(values * values, -1, keepdims=True) + norm_eps)


def norm_backward(values, rate, gain, grads):
    scaled = grads * gain
    value_grad = rate * scaled - values * rate * rate * rate * jnp.mean(
        values * scaled, -1, keepdims=True
    )
    gain_grad = jnp.sum(grads * values * rate, 0)
    return (value_grad, gain_grad)


def dot(left, right):
    return jnp.dot(left, right, preferred_element_type=jnp.float32)


def dot_back(grads, matrix):
    return lax.dot_general(
        grads, matrix, (((1,), (1,)), ((), ())), preferred_element_type=jnp.float32
    )


def dot_grad(rows, grads):
    return lax.dot_general(
        rows, grads, (((0,), (0,)), ((), ())), preferred_element_type=jnp.float32
    )


def share(values):
    return lax.all_gather(values, "dp", axis=0, tiled=True)


def total(values):
    return lax.psum_scatter(
        values.astype(jnp.bfloat16), "dp", scatter_dimension=0, tiled=True
    ).astype(jnp.float32)


MESH = pl.DeviceIdType.MESH
ANY = pl.BlockSpec(memory_space=pl.ANY)


def flip(index, part):
    chip, core = index // 2, index % 2
    return (chip + part // 2) % 2 * 2 + (core + part % 2) % 2


def remote(source, target, sent, landed, **device):
    return pltpu.make_async_remote_copy(
        src_ref=source,
        dst_ref=target,
        send_sem=sent,
        recv_sem=landed,
        device_id=device,
        device_id_type=MESH,
    )


def greet(line, z, y, j, w):
    barrier = pltpu.get_barrier_semaphore()
    for part in range(1, 4):
        pl.semaphore_signal(barrier, device_id={"dp": flip(j, part)}, device_id_type=MESH)
    pl.semaphore_signal(barrier, device_id={"wide": w + 1 - 2 * y}, device_id_type=MESH)

    @pl.when(z > 0)
    def _():
        pl.semaphore_signal(barrier, device_id={"wide": w - 2}, device_id_type=MESH)

    @pl.when(z < line - 1)
    def _():
        pl.semaphore_signal(barrier, device_id={"wide": w + 2}, device_id_type=MESH)

    ends = jnp.where(z > 0, 1, 0) + jnp.where(z < line - 1, 1, 0)
    pl.semaphore_wait(barrier, 4 + ends)


def each(count, step):
    def body(index, carry):
        step(index)
        return carry

    lax.fori_loop(0, count, body, 0)


def gather_kernel(line, half, *refs):
    sent_in, (residual_ref, scale_ref, gain_ref) = refs[:6], refs[6:9]
    outs, (qkv_out, attn_out, middle_out, normed_out) = refs[9:13], refs[13:17]
    rows_out, tables_out = refs[17:19]
    rows_v, tables_v, wqkv_v, wout_v, qkv_v, attn_v, part_v, sum_v, normed_v = refs[19:28]
    loc, dp_send, dp_recv, up_sem, dn_sem, y_sem, recv, keep, sum_send, sum_recv, norm_send, norm_recv = refs[28:]
    qkv_s, out_s, ffn_s = sent_in[:3]
    qkv, out, ffn, low_out = outs
    row_to = (rows_v, low_out, tables_v)
    f32, low = jnp.float32, jnp.bfloat16
    j, w = lax.axis_index("dp"), lax.axis_index("wide")
    z, y = w // 2, w % 2
    other = w + 1 - 2 * y
    greet(line, z, y, j, w)

    def row_copy(part, place):
        there = row_to[place].at[flip(j, 2) if part == 3 else j]
        return remote(
            there if part == 3 else sent_in[3 + place],
            there,
            dp_send.at[3 + place, part],
            dp_recv.at[3 + place, part],
            dp=flip(j, 1 if part == 3 else part),
        )

    def hand_on(place):
        row_copy(2, place).wait_recv()
        row_copy(3, place).start()

    def weight_copy(part, place):
        peer = flip(j, part)
        target = (qkv.at[:, j, w], out.at[j, w], ffn.at[:, j, w])[place]
        return remote(
            sent_in[place].at[peer], target, dp_send.at[place, part], dp_recv.at[place, part], dp=peer
        )

    copies = [
        pltpu.make_async_copy(qkv_s.at[j], qkv.at[:, j, w], loc.at[0]),
        pltpu.make_async_copy(out_s.at[j], out.at[j, w], loc.at[1]),
        pltpu.make_async_copy(ffn_s.at[j], ffn.at[:, j, w], loc.at[2]),
    ] + [
        pltpu.make_async_copy(sent_in[3 + place], row_to[place].at[j], loc.at[3 + place])
        for place in range(3)
    ]
    for copy in copies:
        copy.start()
    for place in range(2):
        for part in range(1, 4):
            weight_copy(part, place).start()

    chunks = []
    for part in range(4):
        chunks += [("qkv", part, 0), ("out", part, 0)]
        if part == 0:
            chunks += [("ffn", 0, 0)]
    chunks += [("ffn", 0, 1)]
    for part in range(1, 4):
        chunks += [("ffn", part, 0), ("ffn", part, 1)]
    count = len(chunks)

    def crosses_first(at):
        name, part, _ = chunks[at]
        return name == "ffn" and part == 0

    def view(at, origin):
        name, part, side = chunks[at]
        if name == "qkv":
            return qkv.at[:, flip(j, part), origin]
        if name == "out":
            return out.at[flip(j, part), origin]
        return ffn.at[:, flip(j, part), origin, :, side * half : (side + 1) * half]

    def up(at, origin):
        there = view(at, origin)
        return remote(there, there, up_sem.at[at, origin], recv.at[at, origin], wide=w + 2)

    def dn(at, origin):
        there = view(at, origin)
        return remote(there, there, dn_sem.at[at, origin], recv.at[at, origin], wide=w - 2)

    def across(at, origin):
        there = view(at, origin)
        return remote(there, there, y_sem.at[at, origin], recv.at[at, origin], wide=other)

    def arrived(at, origin):
        across(at, origin).wait_recv()

    start = lambda copy: copy.start()
    finish = lambda copy: copy.wait_send()

    def both_ways(at, origin, act):
        @pl.when(z < line - 1)
        def _():
            act(up(at, origin))

        @pl.when(z > 0)
        def _():
            act(dn(at, origin))

    waited = []

    def own(at):
        name, part, side = chunks[at]
        place = ("qkv", "out", "ffn").index(name)
        if (place, part) not in waited:
            waited.append((place, part))
            if part == 0:
                copies[place].wait()
            else:
                weight_copy(part, place).wait_recv()
        across(at, w).start()
        both_ways(at, w, start)

    def turn(at):
        arrived(at, other)
        both_ways(at, other, start)

    def pass_on(at, far, act, waiting):
        first = crosses_first(at)
        for side in (0, 1) if first else (0,):
            column = y if side == 0 else 1 - y

            @pl.when(z >= far)
            def _():
                origin = (z - far) * 2 + column
                if waiting:
                    arrived(at, origin)

                @pl.when(z < line - 1)
                def _():
                    act(up(at, origin))

                if not first:
                    act(across(at, origin))

            @pl.when(z + far < line)
            def _():
                origin = (z + far) * 2 + column
                if waiting:
                    arrived(at, origin)

                @pl.when(z > 0)
                def _():
                    act(dn(at, origin))

                if not first:
                    act(across(at, origin))

    heads = attn_v.shape[2] // HD
    seq = rows_v.shape[1]
    turns = (3, 2, 1, 0)
    attn_chunks = [at for at in range(count) if chunks[at][0] in ("qkv", "out")]
    loads = [
        pltpu.make_async_copy(qkv, wqkv_v, keep.at[0]),
        pltpu.make_async_copy(out, wout_v, keep.at[1]),
    ]

    def weights_ready():
        for at in attn_chunks:
            for far in range(line):
                arrived(at, far * 2 + 1 - y)
        for load in loads:
            load.start()
        for part in (1, 3):
            row_copy(part, 0).wait_recv()
            row_copy(part, 2).wait_recv()
        copies[3].wait()
        copies[5].wait()
        for load in loads:
            load.wait()

    def project(part):
        n = flip(j, part)
        cosine, sine = tables_v[n, 0], tables_v[n, 1]
        weights = wqkv_v[...].reshape(D, wqkv_v.shape[4])
        value = jnp.dot(rows_v[n], weights, preferred_element_type=f32)
        for head in range(heads + 1):
            one = value[:, head * HD : (head + 1) * HD]
            turned = one * cosine + pltpu.roll(one, HD // 2, 1) * sine
            qkv_v[part, :, head * HD : (head + 1) * HD] = turned.astype(low)
        qkv_v[part, :, (heads + 1) * HD :] = value[:, (heads + 1) * HD :].astype(low)

    def attend(part, head):
        query = qkv_v[part, :, head * HD : (head + 1) * HD]
        key = qkv_v[part, :, heads * HD : (heads + 1) * HD]
        scores = lax.dot_general(
            query, key, (((1,), (1,)), ((), ())), preferred_element_type=f32
        ) * HD ** (-0.5)
        row = lax.broadcasted_iota(jnp.int32, (seq, seq), 0)
        column = lax.broadcasted_iota(jnp.int32, (seq, seq), 1)
        scores = jnp.where(row >= column, scores, masked_value)
        weight = jnp.exp(scores - jnp.max(scores, -1, keepdims=True))
        probs = (weight / jnp.sum(weight, -1, keepdims=True)).astype(low)
        value = jnp.dot(probs, qkv_v[part, :, (heads + 1) * HD :], preferred_element_type=f32)
        attn_v[part, :, head * HD : (head + 1) * HD] = value.astype(low)

    def send_sum(part):
        peer = flip(j, 1 if part == 3 else part)
        return remote(
            part_v.at[part], sum_v.at[part], sum_send.at[part], sum_recv.at[part], dp=peer
        )

    def finished(part):
        n = flip(j, part)
        return [
            pltpu.make_async_copy(qkv_v.at[part], qkv_out.at[n], keep.at[2 + part]),
            pltpu.make_async_copy(attn_v.at[part], attn_out.at[n], keep.at[6 + part]),
        ]

    def project_out(part):
        weights = wout_v[...].reshape(heads * HD, D)
        if part == 2:
            send_sum(3).wait_recv()
        for cut in range(4):
            columns = slice(cut * D // 4, (cut + 1) * D // 4)
            value = jnp.dot(attn_v[part], weights[:, columns], preferred_element_type=f32)
            if part == 2:
                value = value + sum_v[3, :, columns].astype(f32)
            part_v[part, :, columns] = value.astype(low)
        if part > 0:
            send_sum(part).start()
        for copy in finished(part):
            copy.start()

    def send_normed(part):
        there = normed_out.at[flip(j, 2) if part == 3 else j]
        return remote(
            there if part == 3 else normed_v,
            there,
            norm_send.at[part],
            norm_recv.at[part],
            dp=flip(j, 1 if part == 3 else part),
        )

    keep_normed = pltpu.make_async_copy(normed_v, normed_out.at[j], keep.at[10])
    keep_rows = pltpu.make_async_copy(rows_v, rows_out, keep.at[11])
    keep_tables = pltpu.make_async_copy(tables_v, tables_out, keep.at[12])

    def normalize():
        for part in (1, 2):
            send_sum(part).wait_recv()
        scale = scale_ref[0, 0]

        def rows(index):
            here = pl.ds(pl.multiple_of(index * 32, 32), 32)
            total_rows = part_v[0, here, :].astype(f32)
            for part in (1, 2):
                total_rows = total_rows + sum_v[part, here, :].astype(f32)
            middle = residual_ref[here, :].astype(f32) + scale * total_rows
            middle_out[here, :] = middle
            rate = lax.rsqrt(jnp.mean(middle * middle, -1, keepdims=True) + norm_eps)
            normed_v[here, :] = (middle * rate * gain_ref[...]).astype(low)

        each(seq // 32, rows)
        for part in (1, 2):
            send_normed(part).start()
        keep_normed.start()
        keep_rows.start()
        keep_tables.start()

    work = [weights_ready]
    for part in turns:
        work.append(functools.partial(project, part))
        for head in range(heads):
            work.append(functools.partial(attend, part, head))
        work.append(functools.partial(project_out, part))
    work.append(normalize)
    ready = attn_chunks[-1] + line + 1

    def compute(pieces):
        for _ in range(pieces):
            if work:
                work.pop(0)()

    for step in range(count + line):
        if step < count:
            own(step)
        for far in range(1, line):
            at = step - far - 1
            if 0 <= at < count:
                if far == 1 and crosses_first(at):
                    turn(at)
                pass_on(at, far, start, True)
                if step >= ready:
                    compute(2)
        if step == 2:
            for part in range(1, 4):
                weight_copy(part, 2).start()
        if step == attn_chunks[-1]:
            for part in (1, 2):
                row_copy(part, 0).start()
                row_copy(part, 2).start()
        if step == attn_chunks[-1] + 2:
            for part in (1, 2):
                row_copy(part, 1).start()
        if step == ready - 1:
            hand_on(0)
            hand_on(2)
        if step >= ready:
            compute(2)
        if step == count + 1:
            hand_on(1)
    compute(len(work))
    send_normed(2).wait_recv()
    send_normed(3).start()

    for at in range(count):
        if not crosses_first(at) and at not in attn_chunks:
            for far in range(line):
                arrived(at, far * 2 + 1 - y)
    copies[4].wait()
    for place in range(3):
        for part in range(1, 4):
            if place == 1 and part != 2:
                row_copy(part, place).wait()
            else:
                row_copy(part, place).wait_send()
            weight_copy(part, place).wait_send()
    for at in range(count):
        across(at, w).wait_send()
        both_ways(at, w, finish)
        if crosses_first(at):
            both_ways(at, other, finish)
        for far in range(1, line):
            pass_on(at, far, finish, False)
    for part in range(4):
        for copy in finished(part):
            copy.wait()
        if part > 0:
            send_sum(part).wait_send()
            send_normed(part).wait_send()
        if part in (1, 3):
            send_normed(part).wait_recv()
    keep_normed.wait()
    keep_rows.wait()
    keep_tables.wait()


def gather_call(line, qkv_s, out_s, ffn_s, rows, low_rows, tables, residual, scale, gain):
    low = jnp.bfloat16
    ndp, wide = qkv_s.shape[0], 2 * line
    rm, piece = qkv_s.shape[1], qkv_s.shape[2]
    seq, wq = rows.shape[0], D // ndp

    def shape(*dims, kind=low):
        return jax.ShapeDtypeStruct(dims, kind)

    outs = (
        shape(rm, ndp, wide, piece, qkv_s.shape[3]),
        shape(ndp, wide, piece, out_s.shape[2]),
        shape(rm, ndp, wide, piece, ffn_s.shape[3]),
        shape(ndp, seq, D),
        shape(ndp, seq, qkv_s.shape[3]),
        shape(ndp, seq, wq),
        shape(seq, D, kind=jnp.float32),
        shape(ndp, seq, D),
        shape(ndp, seq, D),
        shape(ndp, *tables.shape, kind=tables.dtype),
    )
    dma = pltpu.SemaphoreType.DMA
    whole = pl.BlockSpec(memory_space=pltpu.VMEM)
    args = (qkv_s, out_s, ffn_s, rows, low_rows, tables)
    count = 16
    return pl.pallas_call(
        functools.partial(gather_kernel, line, ffn_s.shape[3] // 2),
        out_shape=outs,
        in_specs=[ANY] * len(args) + [whole, pl.BlockSpec(memory_space=pltpu.SMEM), whole],
        out_specs=[ANY] * 6 + [whole] + [ANY] * 3,
        scratch_shapes=[
            pltpu.VMEM((ndp, seq, D), low),
            pltpu.VMEM((ndp, *tables.shape), tables.dtype),
            pltpu.VMEM(outs[0].shape, low),
            pltpu.VMEM(outs[1].shape, low),
            pltpu.VMEM((ndp, seq, qkv_s.shape[3]), low),
            pltpu.VMEM((ndp, seq, wq), low),
            pltpu.VMEM((ndp, seq, D), low),
            pltpu.VMEM((ndp, seq, D), low),
            pltpu.VMEM((seq, D), low),
            dma((7,)),
            dma((6, 4)),
            dma((6, 4)),
        ]
        + [dma((count, wide))] * 4
        + [dma((13,)), dma((4,)), dma((4,)), dma((4,)), dma((4,))],
        compiler_params=pltpu.CompilerParams(
            collective_id=0, has_side_effects=True, vmem_limit_bytes=56 * 1024 * 1024
        ),
        name="gather_weights",
    )(*args, residual, scale, gain)


def scatter_kernel(line, half, *refs):
    (grad_ffn, normed_part, middle_in, cotangent, residual, w_out, w_qkv) = refs[:7]
    packed_in, attn_in, rows_in, tables_in, scale_ref, gains_ref = refs[7:13]
    outs, (input_grad, gain_parts) = refs[13:16], refs[16:18]
    crossed, lined, mine_ffn = refs[18:21], refs[21:24], refs[24]
    early, early_line, early_cross = refs[25:28]
    middle_v, late_v, sum_v, part_v, proj_v, wout_v, wqkv_v, wgrad_v, packed_v, tables_v, out_v, kv_v = refs[28:40]
    y_send, y_recv, load, up_sem, dn_sem, recv, dp_send, dp_recv, loc = refs[40:49]
    keep, two_send, two_recv, proj_send, proj_recv, one_send, one_recv = refs[49:]
    j, w = lax.axis_index("dp"), lax.axis_index("wide")
    z, y = w // 2, w % 2
    other = w + 1 - 2 * y
    greet(line, z, y, j, w)
    f32, low = jnp.float32, jnp.bfloat16
    window = 2

    chunks = [("early", 0, 0), ("early", 0, 1)]
    for part in range(1, 4):
        chunks += [("ffn", part, 0), ("ffn", part, 1)]
    for part in range(4):
        chunks += [("qkv", part, 0)]
    for part in range(4):
        chunks += [("out", part, 0)]
    count = len(chunks)
    names = ("qkv", "out", "ffn")

    def source(at, side):
        name, part, cut = chunks[at]
        if name == "qkv":
            return wgrad_v.at[:, flip(j, part), :, side]
        if name == "out":
            return wout_v.at[pl.ds(flip(j, part), 1), :, side]
        return grad_ffn.at[:, flip(j, part), :, side, :, cut * half : (cut + 1) * half]

    def held(refs, at):
        name, part, cut = chunks[at]
        ref = refs[names.index(name)]
        if name == "ffn":
            return ref.at[part - 1, :, :, :, cut * half : (cut + 1) * half]
        return ref.at[part]

    def own_rows(at):
        name, part, cut = chunks[at]
        if name == "ffn":
            return mine_ffn.at[(2 * part + cut) % (window + 2)]
        return source(at, y)

    def cross(at):
        return remote(
            source(at, 1 - y), held(crossed, at), y_send.at[at], y_recv.at[at], wide=other
        )

    def fetch(at):
        cut = chunks[at][2]
        if chunks[at][0] == "early":
            there = grad_ffn.at[:, j, :, :, :, cut * half : (cut + 1) * half]
            return pltpu.make_async_copy(there, early.at[cut], load.at[at])
        return pltpu.make_async_copy(source(at, y), own_rows(at), load.at[at])

    def fetches(at):
        return chunks[at][0] in ("early", "ffn")

    def cross_early(at):
        cut = chunks[at][2]
        return remote(
            early.at[cut, :, z, 1 - y], early_cross.at[cut], y_send.at[at], y_recv.at[at], wide=other
        )

    def moving(at, dest):
        if chunks[at][0] == "early":
            return early.at[chunks[at][2], :, dest]
        return held(crossed, at).at[:, dest]

    def landing(at, put):
        if chunks[at][0] == "early":
            return early_line.at[chunks[at][2], :, put]
        return held(lined, at).at[:, put]

    def up(at, dest, last):
        put = line if last else dest
        return remote(
            moving(at, dest), landing(at, put), up_sem.at[at, dest], recv.at[at, put], wide=w + 2
        )

    def dn(at, dest):
        return remote(
            moving(at, dest), landing(at, dest), dn_sem.at[at, dest], recv.at[at, dest], wide=w - 2
        )

    def arrived(at, put):
        there = landing(at, put)
        remote(there, there, dn_sem.at[at, 0], recv.at[at, put], wide=other).wait_recv()

    def add(at, dest, puts):
        name, part, cut = chunks[at]
        if name == "early":
            if not puts:
                return

            def rows(index):
                for side in range(2):
                    value = early[cut, index, dest, side].astype(f32)
                    for put in puts:
                        value = value + early_line[cut, index, put, side].astype(f32)
                    early[cut, index, dest, side] = value.astype(low)

            each(early.shape[1], rows)
            return
        here, own, line_in = held(crossed, at), own_rows(at), held(lined, at)

        def rows(index):
            value = here[index, dest].astype(f32) + own[index, dest].astype(f32)
            for put in puts:
                value = value + line_in[index, put].astype(f32)
            here[index, dest] = value.astype(low)

        each(here.shape[0], rows)

    def along(at, act):
        for far in range(line - 1, 0, -1):

            @pl.when(z >= far)
            def _():
                dest = z - far
                if act:

                    @pl.when(z < line - 1)
                    def _():
                        arrived(at, dest)
                        add(at, dest, (dest,))

                    @pl.when(z == line - 1)
                    def _():
                        add(at, dest, ())

                    dn(at, dest).start()
                else:
                    dn(at, dest).wait_send()

            @pl.when(z + far < line)
            def _():
                dest = z + far
                if act:

                    @pl.when(z > 0)
                    def _():
                        arrived(at, dest)
                        add(at, dest, (dest,))

                    @pl.when(z == 0)
                    def _():
                        add(at, dest, ())

                    up(at, dest, far == 1).start()
                else:
                    up(at, dest, far == 1).wait_send()

    def collect(at):
        @pl.when(z == 0)
        def _():
            arrived(at, z)
            add(at, z, (z,))

        @pl.when(z == line - 1)
        def _():
            arrived(at, line)
            add(at, z, (line,))

        @pl.when((z > 0) & (z < line - 1))
        def _():
            arrived(at, z)
            arrived(at, line)
            add(at, z, (z, line))

    def give(at):
        name, part, cut = chunks[at]
        rows = held(crossed, at).at[:, z]
        ref = outs[names.index(name)]
        if name == "out":
            target = ref.at[pl.ds(j, 1)]
        elif name == "qkv":
            target = ref.at[j]
        else:
            target = ref.at[j, :, :, cut * half : (cut + 1) * half]
        if part == 0:
            return pltpu.make_async_copy(rows, target, loc.at[at])
        return remote(rows, target, dp_send.at[at], dp_recv.at[at], dp=flip(j, part))

    def give_early(at):
        cut = chunks[at][2]
        target = outs[2].at[j, :, :, cut * half : (cut + 1) * half]
        return pltpu.make_async_copy(early_cross.at[cut], target, loc.at[at])

    def collect_and_give(at):
        collect(at)
        if chunks[at][0] == "early":
            cross_early(at).start()
        else:
            give(at).start()

    def finish_early(at):
        cut = chunks[at][2]
        cross_early(at).wait_recv()

        def rows(index):
            value = early_cross[cut, index].astype(f32) + early[cut, index, z, y].astype(f32)
            early_cross[cut, index] = value.astype(low)

        each(early.shape[1], rows)
        give_early(at).start()

    heads = out_v.shape[1] // HD
    seq = middle_v.shape[0]
    wide_rows = heads * HD
    loads = [
        pltpu.make_async_copy(middle_in, middle_v, keep.at[0]),
        pltpu.make_async_copy(cotangent, late_v, keep.at[1]),
        pltpu.make_async_copy(normed_part.at[j], part_v.at[0], keep.at[2]),
        pltpu.make_async_copy(normed_part.at[flip(j, 2)], part_v.at[2], keep.at[3]),
        pltpu.make_async_copy(w_out, wout_v, keep.at[4]),
        pltpu.make_async_copy(w_qkv, wqkv_v, keep.at[5]),
        pltpu.make_async_copy(packed_in, packed_v, keep.at[6]),
        pltpu.make_async_copy(tables_in, tables_v, keep.at[7]),
    ]
    load_rows = pltpu.make_async_copy(rows_in, part_v, keep.at[8])
    load_attn = [
        pltpu.make_async_copy(
            attn_in.at[n], late_v.at[:, n * wide_rows : (n + 1) * wide_rows], keep.at[9 + n]
        )
        for n in range(4)
    ]
    load_residual = pltpu.make_async_copy(residual, late_v, keep.at[13])
    keep_input = pltpu.make_async_copy(late_v, input_grad, keep.at[14])

    def send_two(part):
        block = part_v.at[2] if part == 2 else normed_part.at[flip(j, part)]
        peer = flip(j, 1 if part == 3 else part)
        return remote(block, sum_v.at[part - 1], two_send.at[part], two_recv.at[part], dp=peer)

    def send_one(part):
        peer = flip(j, 1 if part == 3 else part)
        return remote(
            part_v.at[part], sum_v.at[part - 1], one_send.at[part], one_recv.at[part], dp=peer
        )

    def send_proj(part):
        there = proj_v.at[flip(j, 2) if part == 3 else j]
        peer = flip(j, 1 if part == 3 else part)
        return remote(there, there, proj_send.at[part], proj_recv.at[part], dp=peer)

    def over_rows(step):
        each(seq // 32, lambda index: step(pl.ds(pl.multiple_of(index * 32, 32), 32)))

    def add_two():
        loads[3].wait()
        send_two(3).wait_recv()

        def rows(here):
            value = part_v[2, here, :].astype(f32) + sum_v[2, here, :].astype(f32)
            part_v[2, here, :] = value.astype(low)

        over_rows(rows)
        send_two(2).start()

    def norm_back(values, grads, gain, gain_row):
        rate = lax.rsqrt(jnp.mean(values * values, -1, keepdims=True) + norm_eps)
        scaled = grads * gain
        mean = jnp.mean(values * scaled, -1, keepdims=True)
        gain_parts[gain_row : gain_row + 1, :] += jnp.sum(grads * values * rate, 0, keepdims=True)
        return rate * scaled - values * rate * rate * rate * mean

    def second_norm():
        for at in (0, 1, 2):
            loads[at].wait()
        send_two(1).wait_recv()
        send_two(2).wait_recv()
        gain_parts[...] = jnp.zeros_like(gain_parts)
        scale = scale_ref[0, 0]

        def rows(here):
            grads = part_v[0, here, :].astype(f32)
            for part in (1, 2):
                grads = grads + sum_v[part - 1, here, :].astype(f32)
            value_grad = norm_back(middle_v[here, :], grads, gains_ref[1:2, :], 1)
            middle_grad = late_v[here, :].astype(f32) + value_grad
            middle_v[here, :] = middle_grad
            proj_v[j, here, :] = (scale * middle_grad).astype(low)

        over_rows(rows)
        send_proj(1).start()
        send_proj(2).start()
        send_two(2).wait_send()
        load_rows.start()
        for copy in load_attn:
            copy.start()

    def hand_on():
        send_proj(2).wait_recv()
        send_proj(3).start()

    def out_back(part):
        if part == 0:
            for at in (4, 5, 6, 7):
                loads[at].wait()
        elif part != 2:
            send_proj(part).wait_recv()
        weights = wout_v[...].reshape(wide_rows, D)
        value = lax.dot_general(
            proj_v[flip(j, part)], weights, (((1,), (1,)), ((), ())), preferred_element_type=f32
        )
        out_v[...] = value.astype(low)

    def turn_back(values, n):
        return values * tables_v[n, 0] - pltpu.roll(values, HD // 2, 1) * tables_v[n, 1]

    def attend_back(part, head):
        n = flip(j, part)
        own = slice(head * HD, (head + 1) * HD)
        query = packed_v[n, :, own]
        key = packed_v[n, :, wide_rows : wide_rows + HD]
        value = packed_v[n, :, wide_rows + HD :]
        grad = out_v[:, own]
        scores = lax.dot_general(
            query, key, (((1,), (1,)), ((), ())), preferred_element_type=f32
        ) * HD ** (-0.5)
        row = lax.broadcasted_iota(jnp.int32, (seq, seq), 0)
        column = lax.broadcasted_iota(jnp.int32, (seq, seq), 1)
        scores = jnp.where(row >= column, scores, masked_value)
        weight = jnp.exp(scores - jnp.max(scores, -1, keepdims=True))
        probs = weight / jnp.sum(weight, -1, keepdims=True)
        prob_grads = lax.dot_general(
            grad, value, (((1,), (1,)), ((), ())), preferred_element_type=f32
        )
        row_dot = jnp.sum(prob_grads * probs, -1, keepdims=True)
        score_low = (probs * (prob_grads - row_dot)).astype(low)
        query_grad = jnp.dot(score_low, key, preferred_element_type=f32) * HD ** (-0.5)
        key_grad = lax.dot_general(
            score_low, query, (((0,), (0,)), ((), ())), preferred_element_type=f32
        ) * HD ** (-0.5)
        value_grad = lax.dot_general(
            probs.astype(low), grad, (((0,), (0,)), ((), ())), preferred_element_type=f32
        )
        if head == 0:
            kv_v[0] = key_grad
            kv_v[1] = value_grad
        else:
            kv_v[0] += key_grad
            kv_v[1] += value_grad
        packed_v[n, :, own] = turn_back(query_grad, n).astype(low)
        if head == heads - 1:
            packed_v[n, :, wide_rows : wide_rows + HD] = turn_back(kv_v[0], n).astype(low)
            packed_v[n, :, wide_rows + HD :] = kv_v[1].astype(low)

    def out_grad(cut):
        if cut == 0:
            for copy in load_attn:
                copy.wait()
        columns = slice(cut * D // 4, (cut + 1) * D // 4)
        rows = jnp.concatenate(
            [late_v[:, n * wide_rows : (n + 1) * wide_rows] for n in range(4)], 0
        )
        grads = proj_v[:, :, columns].reshape(4 * seq, D // 4)
        value = lax.dot_general(rows, grads, (((0,), (0,)), ((), ())), preferred_element_type=f32)
        shape = wout_v.shape[:-1] + (D // 4,)
        wout_v[:, :, :, :, columns] = value.astype(low).reshape(shape)

    def qkv_grad(cut):
        if cut == 0:
            load_rows.wait()
            load_residual.start()
        columns = slice(cut * D // 4, (cut + 1) * D // 4)
        rows = part_v[:, :, columns].reshape(4 * seq, D // 4)
        grads = packed_v[...].reshape(4 * seq, packed_v.shape[2])
        value = lax.dot_general(rows, grads, (((0,), (0,)), ((), ())), preferred_element_type=f32)
        wgrad_v[cut] = value.astype(low).reshape(wgrad_v.shape[1:])

    def rows_back(part):
        n = flip(j, part)
        if part == 2:
            send_one(3).wait_recv()
        for cut in range(4):
            columns = slice(cut * D // 4, (cut + 1) * D // 4)
            weights = wqkv_v[cut].reshape(D // 4, packed_v.shape[2])
            value = lax.dot_general(
                packed_v[n], weights, (((1,), (1,)), ((), ())), preferred_element_type=f32
            )
            if part == 2:
                value = value + sum_v[2, :, columns].astype(f32)
            part_v[part, :, columns] = value.astype(low)
        if part > 0:
            send_one(part).start()

    def first_norm():
        load_residual.wait()
        for part in (1, 2):
            send_one(part).wait_recv()

        def rows(here):
            grads = part_v[0, here, :].astype(f32)
            for part in (1, 2):
                grads = grads + sum_v[part - 1, here, :].astype(f32)
            value_grad = norm_back(late_v[here, :].astype(f32), grads, gains_ref[0:1, :], 0)
            late_v[here, :] = (middle_v[here, :] + value_grad).astype(low)

        over_rows(rows)
        keep_input.start()

    def sequence(part):
        return [functools.partial(out_back, part)] + [
            functools.partial(attend_back, part, head) for head in range(heads)
        ]

    work = {
        1: [second_norm] + sequence(0),
        2: sequence(1) + [hand_on],
        3: sequence(3) + sequence(2),
        4: [functools.partial(out_grad, cut) for cut in range(4)]
        + [functools.partial(qkv_grad, cut) for cut in range(4)],
        7: [functools.partial(rows_back, 3)],
        8: [functools.partial(rows_back, 2)],
        9: [functools.partial(rows_back, 1)],
        10: [functools.partial(rows_back, 0)],
        12: [first_norm],
    }

    late = list(range(2, count))
    send_two(3).start()
    send_two(1).start()
    for at in range(2):
        fetch(at).start()
    for copy in loads:
        copy.start()

    def begin(at):
        if fetches(at):
            fetch(at).start()
        cross(at).start()

    for at in late[:window]:
        begin(at)
    add_two()
    for at in range(2):
        fetch(at).wait()
        along(at, True)
    for step, at in enumerate(late):
        pieces = work.get(step, [])
        cut = (len(pieces) + 1) // 2
        cross(at).wait_send()
        following = late[step + window] if step + window < len(late) else None
        if following is not None and step != 4:
            begin(following)
        cross(at).wait_recv()
        if fetches(at):
            fetch(at).wait()
        along(at, True)
        for piece in pieces[:cut]:
            piece()
        if step < 2:
            collect_and_give(step)
        if step >= 1:
            collect_and_give(late[step - 1])
        for piece in pieces[cut:]:
            piece()
        if step == 4:
            begin(following)
        if step in (3, 4):
            finish_early(step - 3)
    collect_and_give(late[-1])
    for at in range(count):
        along(at, False)
        if chunks[at][0] == "early":
            cross_early(at).wait_send()
            give_early(at).wait()
        else:
            give(at).wait()
    for part in range(1, 4):
        if part != 2:
            send_two(part).wait_send()
        send_proj(part).wait_send()
        send_one(part).wait_send()
    keep_input.wait()


def scatter_call(line, ffn, normed_part, middle, cotangent, residual, w_out, w_qkv, packed, attn, rows, tables, scale, gains):
    low = jnp.bfloat16
    rm, ndp, _, piece, wq = w_qkv.shape
    wf, wo = ffn.shape[4], w_out.shape[3]
    seq = middle.shape[0]
    ffn = ffn.reshape(rm, ndp, line, 2, piece, wf)
    w_out = w_out.reshape(ndp, line, 2, piece, wo)
    w_qkv = w_qkv.reshape(rm, ndp, line, 2, piece, wq)

    def shape(*dims, kind=low):
        return jax.ShapeDtypeStruct(dims, kind)

    outs = (
        shape(ndp, rm, piece, wq),
        shape(ndp, piece, wo),
        shape(ndp, rm, piece, wf),
        shape(seq, D),
        shape(2, D, kind=jnp.float32),
    )

    def held(places):
        return [
            pltpu.VMEM((ndp, rm, places, piece, wq), low),
            pltpu.VMEM((ndp, 1, places, piece, wo), low),
            pltpu.VMEM((ndp - 1, rm, places, piece, wf), low),
        ]

    dma = pltpu.SemaphoreType.DMA
    whole = pl.BlockSpec(memory_space=pltpu.VMEM)
    count = 16
    return pl.pallas_call(
        functools.partial(scatter_kernel, line, wf // 2),
        out_shape=outs,
        in_specs=[ANY] * 11 + [pl.BlockSpec(memory_space=pltpu.SMEM), whole],
        out_specs=[ANY] * 4 + [whole],
        scratch_shapes=held(line)
        + held(line + 1)
        + [
            pltpu.VMEM((4, rm, line, piece, wf // 2), low),
            pltpu.VMEM((2, rm, line, 2, piece, wf // 2), low),
            pltpu.VMEM((2, rm, line + 1, 2, piece, wf // 2), low),
            pltpu.VMEM((2, rm, piece, wf // 2), low),
            pltpu.VMEM((seq, D), jnp.float32),
            pltpu.VMEM((seq, D), low),
            pltpu.VMEM((3, seq, D), low),
            pltpu.VMEM((ndp, seq, D), low),
            pltpu.VMEM((ndp, seq, D), low),
            pltpu.VMEM(w_out.shape, low),
            pltpu.VMEM(w_qkv.shape, low),
            pltpu.VMEM(w_qkv.shape, low),
            pltpu.VMEM(packed.shape, low),
            pltpu.VMEM(tables.shape, tables.dtype),
            pltpu.VMEM((seq, attn.shape[2]), low),
            pltpu.VMEM((2, seq, HD), jnp.float32),
        ]
        + [dma((count,))] * 3
        + [dma((count, line)), dma((count, line)), dma((count, line + 1))]
        + [dma((count,))] * 3
        + [dma((15,))]
        + [dma((4,))] * 6,
        compiler_params=pltpu.CompilerParams(
            collective_id=1, has_side_effects=True, vmem_limit_bytes=60 * 1024 * 1024
        ),
        name="scatter_grads",
    )(ffn, normed_part, middle, cotangent, residual, w_out, w_qkv, packed, attn, rows, tables, scale, gains)


def gains_kernel(line, part_ref, total_ref, dp_parts, wide_parts, dp_send, dp_recv, wide_send, wide_recv):
    j, w = lax.axis_index("dp"), lax.axis_index("wide")
    wide = 2 * line
    barrier = pltpu.get_barrier_semaphore()
    for part in range(1, 4):
        pl.semaphore_signal(barrier, device_id={"dp": flip(j, part)}, device_id_type=MESH)
    for far in range(1, wide):
        pl.semaphore_signal(barrier, device_id={"wide": (w + far) % wide}, device_id_type=MESH)
    pl.semaphore_wait(barrier, 3 + wide - 1)
    copies = [
        remote(part_ref, dp_parts.at[j], dp_send.at[part], dp_recv.at[part], dp=flip(j, part))
        for part in range(1, 4)
    ]
    for copy in copies:
        copy.start()
    dp_parts[j] = part_ref[...]
    for copy in copies:
        copy.wait()
    value = dp_parts[0]
    for rank in range(1, 4):
        value = value + dp_parts[rank]
    wide_parts[w] = value
    copies = [
        remote(
            wide_parts.at[w],
            wide_parts.at[w],
            wide_send.at[far],
            wide_recv.at[far],
            wide=(w + far) % wide,
        )
        for far in range(1, wide)
    ]
    for copy in copies:
        copy.start()
    for copy in copies:
        copy.wait()
    value = wide_parts[0]
    for rank in range(1, wide):
        value = value + wide_parts[rank]
    total_ref[...] = value


def gains_call(line, parts):
    dma = pltpu.SemaphoreType.DMA
    whole = pl.BlockSpec(memory_space=pltpu.VMEM)
    return pl.pallas_call(
        functools.partial(gains_kernel, line),
        out_shape=jax.ShapeDtypeStruct(parts.shape, jnp.float32),
        in_specs=[whole],
        out_specs=whole,
        scratch_shapes=[
            pltpu.VMEM((4, *parts.shape), jnp.float32),
            pltpu.VMEM((2 * line, *parts.shape), jnp.float32),
            dma((4,)),
            dma((4,)),
            dma((2 * line,)),
            dma((2 * line,)),
        ],
        compiler_params=pltpu.CompilerParams(collective_id=2, has_side_effects=True),
        name="sum_gains",
    )(parts)


def attention(tokens, ndp, heads, qkv_rows, tables):
    low = jnp.bfloat16
    seq_len = tokens // ndp
    cosine, sine = tables[:, 0].reshape(tokens, 1, HD), tables[:, 1].reshape(tokens, 1, HD)
    turned = qkv_rows[:, : (heads + 1) * HD].reshape(tokens, heads + 1, HD)
    turned = (turned * cosine + jnp.roll(turned, HD // 2, -1) * sine).astype(low)
    query_rows = turned[:, :heads].reshape(ndp, seq_len, heads, HD)
    key_rows = turned[:, heads].reshape(ndp, seq_len, HD)
    value_rows = qkv_rows[:, (heads + 1) * HD :].astype(low).reshape(ndp, seq_len, HD)
    probs_low = attention_probs(query_rows, key_rows).astype(low)
    out_low = jnp.einsum(
        "ngst,ntd->nsgd", probs_low, value_rows, preferred_element_type=jnp.float32
    ).astype(low)
    packed = jnp.concatenate(
        [turned.reshape(ndp, seq_len, (heads + 1) * HD), value_rows], -1
    )
    return packed, out_low.reshape(ndp, seq_len, heads * HD)


def attention_probs(query_rows, key_rows):
    seq_len = query_rows.shape[1]
    causal = jnp.arange(seq_len)[:, None] >= jnp.arange(seq_len)[None, :]
    scores = jnp.einsum(
        "nsgd,ntd->ngst", query_rows, key_rows, preferred_element_type=jnp.float32
    ) * HD ** (-0.5)
    scores = jnp.where(causal, scores, masked_value)
    row_top = jnp.max(scores, -1, keepdims=True)
    exp_scores = jnp.exp(scores - row_top)
    return exp_scores / jnp.sum(exp_scores, -1, keepdims=True)


def gather_weights(qkv_s, out_s, ffn_s, rows, low_rows, tables, residual, scale, gain):
    ndp, nwide = lax.axis_size("dp"), lax.axis_size("wide")
    if ndp == 4 and nwide == 8 and qkv_s.shape[2] % 16 == 0:
        return gather_call(
            nwide // 2, qkv_s, out_s, ffn_s, rows, low_rows, tables, residual, scale, gain
        )

    def spread(values):
        moved = lax.all_to_all(values, "dp", split_axis=0, concat_axis=0, tiled=True)
        return lax.all_gather(moved, "wide", axis=0)

    seq_len = rows.shape[0]
    tokens = ndp * seq_len
    heads = HEADS // ndp
    w_qkv = spread(qkv_s).transpose(2, 1, 0, 3, 4)
    w_out = spread(out_s).transpose(1, 0, 2, 3)
    w_ffn = spread(ffn_s).transpose(2, 1, 0, 3, 4)
    normed_one = lax.all_gather(rows, "dp", axis=0)
    all_tables = lax.all_gather(tables, "dp", axis=0)
    packed, out_low = attention(
        tokens,
        ndp,
        heads,
        dot(normed_one.reshape(tokens, D), w_qkv.reshape(D, -1)),
        all_tables,
    )
    part = dot(out_low.reshape(tokens, heads * HD), w_out.reshape(heads * HD, D))
    middle = residual.astype(jnp.float32) + scale * total(part)
    normed_two = (middle * norm_rate(middle) * gain).astype(jnp.bfloat16)
    return (
        w_qkv,
        w_out,
        w_ffn,
        lax.all_gather(low_rows, "dp", axis=0),
        packed,
        out_low,
        middle,
        lax.all_gather(normed_two, "dp", axis=0),
        normed_one,
        all_tables,
    )


def scatter_grads(
    ffn, normed_part, middle, cotangent, residual, w_out, w_qkv, packed, attn, rows, tables, scale, gains
):
    ndp, nwide = lax.axis_size("dp"), lax.axis_size("wide")
    if ndp == 4 and nwide == 8 and ffn.shape[3] % 16 == 0:
        return scatter_call(
            nwide // 2, ffn, normed_part, middle, cotangent, residual,
            w_out, w_qkv, packed, attn, rows, tables, scale, gains,
        )
    low = jnp.bfloat16
    _, seq_len, width = packed.shape
    tokens = ndp * seq_len
    heads = HEADS // ndp
    wq = heads * HD
    score_scale = HD ** (-0.5)
    query_rows = packed[..., :wq].reshape(ndp, seq_len, heads, HD)
    key_rows = packed[..., wq : wq + HD]
    value_rows = packed[..., wq + HD :]
    normed_grad = total(normed_part.reshape(tokens, D))
    middle_local, gain_two = norm_backward(middle, norm_rate(middle), gains[1], normed_grad)
    middle_grad = cotangent.astype(jnp.float32) + middle_local
    proj_low = share((scale * middle_grad).astype(low))
    probs_float = attention_probs(query_rows, key_rows)
    attn_grad = dot_back(proj_low, w_out.reshape(wq, D)).astype(low)
    attn_grad = attn_grad.reshape(ndp, seq_len, heads, HD)
    prob_grads = jnp.einsum(
        "nsgd,ntd->ngst", attn_grad, value_rows, preferred_element_type=jnp.float32
    )
    row_dot = jnp.sum(prob_grads * probs_float, -1, keepdims=True)
    score_low = (probs_float * (prob_grads - row_dot)).astype(low)
    query_grad = (
        jnp.einsum("ngst,ntd->nsgd", score_low, key_rows, preferred_element_type=jnp.float32)
        * score_scale
    )
    key_grad = (
        jnp.einsum("ngst,nsgd->ntd", score_low, query_rows, preferred_element_type=jnp.float32)
        * score_scale
    )
    value_grad = jnp.einsum(
        "ngst,nsgd->ntd",
        probs_float.astype(low),
        attn_grad,
        preferred_element_type=jnp.float32,
    )
    turned = jnp.concatenate([query_grad.reshape(ndp, seq_len, wq), key_grad], -1)
    turned = turned.reshape(tokens, heads + 1, HD)
    cosine = tables[:, 0].reshape(tokens, 1, HD)
    sine = tables[:, 1].reshape(tokens, 1, HD)
    turned = (turned * cosine - jnp.roll(turned, HD // 2, -1) * sine).astype(low)
    qkv_low = jnp.concatenate(
        [turned.reshape(tokens, wq + HD), value_grad.reshape(tokens, HD).astype(low)], 1
    )
    normed_grad = total(dot_back(qkv_low, w_qkv.reshape(D, width)))
    source = residual.astype(jnp.float32)
    input_local, gain_one = norm_backward(source, norm_rate(source), gains[0], normed_grad)

    def collect(values):
        moved = lax.psum_scatter(values, "wide", scatter_dimension=0, tiled=False)
        return lax.all_to_all(moved, "dp", split_axis=0, concat_axis=0, tiled=True)

    grad_qkv = dot_grad(rows.reshape(tokens, D), qkv_low).astype(low).reshape(w_qkv.shape)
    grad_out = dot_grad(attn.reshape(tokens, wq), proj_low).astype(low).reshape(w_out.shape)
    return (
        collect(grad_qkv.transpose(2, 1, 0, 3, 4)),
        collect(grad_out.transpose(1, 0, 2, 3)),
        collect(ffn.transpose(2, 1, 0, 3, 4)),
        (middle_grad + input_local).astype(low),
        jnp.stack([gain_one, gain_two]),
    )


def sum_gains(parts):
    ndp, nwide = lax.axis_size("dp"), lax.axis_size("wide")
    if ndp == 4 and nwide == 8:
        return gains_call(nwide // 2, parts)
    return lax.psum(parts, ("dp", "wide"))


def unfold_rows(rows_ref, flat_ref, piece):
    count = rows_ref.shape[0]
    for first in range(0, count, 8):
        size = min(8, count - first)
        for row in range(piece):
            for group in range(B // 128):
                start = row * B + group * 128
                flat_ref[group, pl.ds(first * piece + row, size, stride=piece), :] = rows_ref[
                    first : first + size, start : start + 128
                ]


def block_places(rm, ndp, rf, part):
    places = []
    for i in range(rm):
        for c in range(ndp):
            places.append((i * ndp + c, 0, 0, (c, i), 0, B))
    for i in range(rm):
        for c in range(ndp):
            places.append((rm * rm + i, c * part, 0, (c, i), B, part))
            places.append((rm * rm + rm + i, c * part, 0, (c, i), B + part, part))
    first = rm * rm + 2 * rm
    for c in range(ndp):
        for i in range(rm):
            places.append((first + c * rm + i, 0, 1, (c,), i * B, B))
    first = first + rm * rm
    for i in range(rm):
        for b in range(rf):
            for c in range(ndp):
                for side in range(2):
                    block = first + side * rm * rf + i * rf + b
                    places.append((block, c * part, 2, (c, i), (side * rf + b) * part, part))
    first = first + 2 * rm * rf
    for b in range(rf):
        for i in range(rm):
            places.append((first + b * rm + i, 0, 3, (b,), i * B, B))
    return places


def pack_kernel(places, piece, rows_ref, *refs):
    pieces, flat_ref = refs[:4], refs[4]
    unfold_rows(rows_ref, flat_ref, piece)
    for block, column, array, lead, start, width in places:
        for offset in range(0, width, 128):
            value = flat_ref[(column + offset) // 128, block * piece : (block + 1) * piece, :]
            there = slice(start + offset, start + offset + 128)
            pieces[array][(*lead, slice(None), there)] = value.astype(jnp.bfloat16)


def slots_kernel(places, piece, slot_ref, *refs):
    pieces, send_ref, blocks_ref = refs[:4], refs[4], refs[5]
    for block, column, array, lead, start, width in places:
        value = pieces[array][(*lead, slice(None), slice(start, start + width))]
        blocks_ref[block, :, column : column + width] = value
    each_slot = send_ref.shape[1]

    def device(index, carry):
        for slot in range(each_slot):
            block = slot_ref[index * each_slot + slot]
            value = blocks_ref[jnp.maximum(block, 0)]
            send_ref[index, slot] = jnp.where(block >= 0, value, jnp.zeros_like(value))
        return carry

    lax.fori_loop(0, send_ref.shape[0], device, 0)


def precondition_kernel(scale_ref, grad_ref, left_ref, right_ref, step_ref):
    low, f32 = jnp.bfloat16, jnp.float32
    scale = scale_ref[pl.program_id(0)]
    grad = grad_ref[:, 0].reshape(B, B)
    value = jnp.dot(left_ref[0].astype(low), grad, preferred_element_type=f32)
    value = jnp.dot(value.astype(low), right_ref[0].astype(low), preferred_element_type=f32)
    rate = lax.rsqrt(jnp.mean(value * value, keepdims=True) + scale_eps)
    value = value * (weight_rate * scale * rate)
    step_ref[:, 0] = value.astype(low).reshape(step_ref.shape[0], step_ref.shape[2], B)


def update_kernel(piece, slot_ref, steps_ref, master_ref, out_ref, flat_ref):
    each_slot = steps_ref.shape[1]
    count = master_ref.shape[0]

    def block(index, carry):
        slot = slot_ref[index]
        value = steps_ref[slot // each_slot, slot % each_slot].astype(jnp.float32)
        rows = pl.ds(pl.multiple_of(index * piece, piece), piece)
        for group in range(B // 128):
            flat_ref[group, rows, :] = value[:, group * 128 : (group + 1) * 128]
        return carry

    lax.fori_loop(0, count, block, 0)
    for first in range(0, count, 8):
        size = min(8, count - first)
        for row in range(piece):
            for group in range(B // 128):
                step = flat_ref[group, pl.ds(first * piece + row, size, stride=piece), :]
                start = row * B + group * 128
                columns = slice(start, start + 128)
                out_ref[first : first + size, columns] = (1.0 - weight_decay) * master_ref[
                    first : first + size, columns
                ] - step


def vmem_call(kernel, outs, args, scratch=(), prefetch=0, name=None):
    whole = pl.BlockSpec(memory_space=pltpu.VMEM)
    small = pl.BlockSpec(memory_space=pltpu.SMEM)
    return pl.pallas_call(
        kernel,
        out_shape=outs,
        in_specs=[small] * prefetch + [whole] * (len(args) - prefetch),
        out_specs=jax.tree.map(lambda _: whole, outs),
        scratch_shapes=list(scratch),
        compiler_params=pltpu.CompilerParams(vmem_limit_bytes=48 * 1024 * 1024),
        name=name,
    )(*args)


def pack_call(rows, ndp):
    rm, rf, part, piece = D // B, FF // B, B // ndp, rows.shape[1] // B
    low = jnp.bfloat16
    outs = (
        jax.ShapeDtypeStruct((ndp, rm, piece, B + 2 * part), low),
        jax.ShapeDtypeStruct((ndp, piece, D), low),
        jax.ShapeDtypeStruct((ndp, rm, piece, 2 * rf * part), low),
        jax.ShapeDtypeStruct((rf, piece, D), low),
    )
    return vmem_call(
        functools.partial(pack_kernel, block_places(rm, ndp, rf, part), piece),
        outs,
        (rows,),
        [pltpu.VMEM((B // 128, NBLK * piece, 128), jnp.float32)],
        name="pack",
    )


def slots_call(slot_block, pieces, devices):
    ndp, rm, piece, _ = pieces[0].shape
    rf = pieces[3].shape[0]
    low = jnp.bfloat16
    outs = (
        jax.ShapeDtypeStruct((devices, slot_block.shape[0] // devices, piece, B), low),
        jax.ShapeDtypeStruct((NBLK, piece, B), low),
    )
    return vmem_call(
        functools.partial(slots_kernel, block_places(rm, ndp, rf, B // ndp), piece),
        outs,
        (slot_block, *pieces),
        prefetch=1,
        name="to_slots",
    )


def precondition_call(scale, owned, left, right):
    devices, slots, piece, _ = owned.shape
    block = pl.BlockSpec((devices, 1, piece, B), lambda n: (0, n, 0, 0))
    square = pl.BlockSpec((1, B, B), lambda n: (n, 0, 0))
    return pl.pallas_call(
        precondition_kernel,
        out_shape=jax.ShapeDtypeStruct(owned.shape, jnp.bfloat16),
        grid=(slots,),
        in_specs=[pl.BlockSpec(memory_space=pltpu.SMEM), block, square, square],
        out_specs=block,
        compiler_params=pltpu.CompilerParams(vmem_limit_bytes=48 * 1024 * 1024),
        name="precondition",
    )(scale, owned, left, right)


def update_call(block_slot, returned, master):
    piece = master.shape[1] // B
    return vmem_call(
        functools.partial(update_kernel, piece),
        jax.ShapeDtypeStruct(master.shape, jnp.float32),
        (block_slot, returned, master),
        [pltpu.VMEM((B // 128, NBLK * piece, 128), jnp.float32)],
        prefetch=1,
        name="update",
    )


def pack(master_weights, ndp):
    low = jnp.bfloat16
    piece = master_weights.shape[1] // B
    if ndp == 4 and piece % 16 == 0:
        return pack_call(master_weights, ndp)
    rm, rf, part = D // B, FF // B, B // ndp
    first_key = rm * rm
    first_value = first_key + rm
    first_out = first_value + rm
    first_gate = first_out + rm * rm
    first_up = first_gate + rm * rf
    first_down = first_up + rm * rf
    mine = master_weights.astype(low).reshape(NBLK, piece, B)

    def cut_columns(first, blocks):
        own = mine[first : first + rm * blocks].reshape(rm, blocks, piece, ndp, part)
        return own.transpose(3, 0, 2, 1, 4).reshape(ndp, rm, piece, blocks * part)

    qkv_s = jnp.concatenate(
        [
            mine[:first_key].reshape(rm, ndp, piece, B).transpose(1, 0, 2, 3),
            cut_columns(first_key, 1),
            cut_columns(first_value, 1),
        ],
        -1,
    )
    out_s = (
        mine[first_out:first_gate].reshape(ndp, rm, piece, B).transpose(0, 2, 1, 3)
    ).reshape(ndp, piece, D)
    ffn_s = jnp.concatenate([cut_columns(first_gate, rf), cut_columns(first_up, rf)], -1)
    down_s = mine[first_down:].reshape(rf, rm, piece, B).transpose(0, 2, 1, 3)
    down_s = down_s.reshape(rf, piece, D)
    return qkv_s, out_s, ffn_s, down_s


def to_slots(slot_block, pieces, devices):
    ndp, rm, piece, _ = pieces[0].shape
    if ndp == 4 and piece % 16 == 0:
        return slots_call(slot_block, pieces, devices)
    grad_qkv, grad_out, grad_ffn, grad_down = pieces
    low = jnp.bfloat16
    rf = grad_down.shape[0]
    part = B // ndp
    wq = B

    def join_columns(cut, blocks):
        own = cut.reshape(ndp, rm, piece, blocks, part).transpose(1, 3, 2, 0, 4)
        return own.reshape(rm * blocks, piece, B)

    grad_rows = jnp.concatenate(
        [
            grad_qkv[..., :wq].transpose(1, 0, 2, 3).reshape(rm * ndp, piece, B),
            join_columns(grad_qkv[..., wq : wq + part], 1),
            join_columns(grad_qkv[..., wq + part :], 1),
            grad_out.reshape(ndp, piece, rm, B).transpose(0, 2, 1, 3).reshape(ndp * rm, piece, B),
            join_columns(grad_ffn[..., : rf * part], rf),
            join_columns(grad_ffn[..., rf * part :], rf),
            grad_down.reshape(rf, piece, rm, B).transpose(0, 2, 1, 3).reshape(rf * rm, piece, B),
        ],
        0,
    )
    send_rows = jnp.where(
        (slot_block >= 0)[:, None, None],
        grad_rows[jnp.maximum(slot_block, 0)],
        jnp.zeros((), low),
    )
    return send_rows.reshape(devices, -1, piece, B), grad_rows


def precondition(scale, owned, left, right):
    low = jnp.bfloat16
    devices, slots, piece, _ = owned.shape
    if piece % 16 == 0:
        return precondition_call(scale, owned, left, right)
    blocks = owned.transpose(1, 0, 2, 3).reshape(slots, B, B)
    value = jnp.einsum("nij,njk->nik", left.astype(low), blocks, preferred_element_type=jnp.float32)
    value = jnp.einsum(
        "nij,njk->nik", value.astype(low), right.astype(low), preferred_element_type=jnp.float32
    )
    rate = lax.rsqrt(jnp.mean(value * value, axis=(1, 2), keepdims=True) + scale_eps)
    steps = weight_rate * scale[:, None, None] * value * rate
    return steps.astype(low).reshape(slots, devices, piece, B).transpose(1, 0, 2, 3)


def update(block_slot, returned, master_weights):
    devices, slots, piece, _ = returned.shape
    if piece % 16 == 0:
        return update_call(block_slot, returned, master_weights)
    steps = returned.reshape(devices * slots, piece, B)[block_slot].astype(jnp.float32)
    return (1.0 - weight_decay) * master_weights - steps.reshape(NBLK, piece * B)


def local(
    inputs,
    cotangent,
    keep_mask,
    positions,
    master_weights,
    gains,
    gain_moments,
    block_slot,
    stat_left,
    stat_right,
    root_left,
    root_right,
):
    low = jnp.bfloat16
    ndp = lax.axis_size("dp")
    nwide = lax.axis_size("wide")
    rm = D // B
    rf = FF // B
    seq_len = inputs.shape[1]
    tokens = ndp * seq_len
    slot_dev = stat_left.shape[0]
    slots_all = slot_dev * ndp * nwide
    piece = master_weights.shape[1] // B
    part = B // ndp

    residual = inputs[0].astype(jnp.float32)
    branch_scale = keep_mask[0].astype(jnp.float32) / keep_rate()
    out_grad_f = cotangent[0].astype(jnp.float32)
    rate_one = norm_rate(residual)

    qkv_s, out_s, ffn_s, down_s = pack(master_weights, ndp)
    down_all = lax.all_gather(down_s, "wide", axis=0)
    cosine_table, sine_table = rope_tables(positions[0])
    signs = jnp.where(jnp.arange(HD) < HD // 2, -1.0, 1.0)
    (
        w_qkv,
        w_out,
        w_ffn,
        down_low,
        packed,
        out_low,
        middle,
        normed_two,
        normed_one,
        all_tables,
    ) = gather_weights(
        qkv_s,
        out_s,
        ffn_s,
        (residual * rate_one * gains[0]).astype(low),
        (branch_scale * out_grad_f).astype(low),
        jnp.stack([cosine_table, sine_table * signs]),
        inputs[0],
        branch_scale.reshape(1, 1),
        gains[1:],
    )
    w_ffn = w_ffn.reshape(D, 2 * rf * part)
    w_down = down_all.transpose(1, 0, 2, 3).reshape(rf * part, D)
    normed_two = normed_two.reshape(tokens, D)
    down_low = down_low.reshape(tokens, D)

    ffn_rows = dot(normed_two, w_ffn)
    gate_rows, up_rows = ffn_rows[:, : rf * part], ffn_rows[:, rf * part :]
    sigmoid_gate = jax.nn.sigmoid(gate_rows)
    hidden = (gate_rows * sigmoid_gate * up_rows).astype(low)
    hidden_grad = dot_back(down_low, w_down)
    gate_low = (
        hidden_grad * up_rows * sigmoid_gate * (1.0 + gate_rows * (1.0 - sigmoid_gate))
    ).astype(low)
    up_low = (hidden_grad * gate_rows * sigmoid_gate).astype(low)
    ffn_low = jnp.concatenate([gate_low, up_low], 1)
    down_part = dot_grad(hidden, down_low).astype(low).reshape(rf, nwide, piece, D)
    down_part, ffn_low = lax.optimization_barrier((down_part.transpose(1, 0, 2, 3), ffn_low))
    grad_down = lax.psum_scatter(down_part, "wide", scatter_dimension=0, tiled=False)
    result = middle + branch_scale * total(dot(hidden, w_down))
    output = result.astype(low)[None]
    grad_qkv, grad_out, grad_ffn, input_grad, gain_parts = scatter_grads(
        dot_grad(normed_two, ffn_low).astype(low).reshape(rm, ndp, nwide, piece, 2 * rf * part),
        dot_back(ffn_low, w_ffn).astype(low).reshape(ndp, seq_len, D),
        middle,
        cotangent[0],
        inputs[0],
        w_out,
        w_qkv,
        packed,
        out_low,
        normed_one,
        all_tables,
        branch_scale.reshape(1, 1),
        gains,
    )
    input_grad = input_grad[None]
    gain_grads = sum_gains(gain_parts)
    new_gain_moments = stat_decay * gain_moments + (1.0 - stat_decay) * gain_grads * gain_grads
    new_gains = gains - gain_rate * gain_grads / (jnp.sqrt(new_gain_moments) + adam_eps)

    slot_block = jnp.full((slots_all,), -1, jnp.int32).at[block_slot].set(jnp.arange(NBLK))
    send_rows, grad_rows = to_slots(
        slot_block, (grad_qkv, grad_out, grad_ffn, grad_down), ndp * nwide
    )
    grad_local = grad_rows.reshape(NBLK, piece * B).astype(jnp.float32)
    owned = lax.all_to_all(send_rows, ("dp", "wide"), split_axis=0, concat_axis=0, tiled=True)
    own_blocks = lax.dynamic_slice_in_dim(
        slot_block, lax.axis_index(("dp", "wide")) * slot_dev, slot_dev
    )
    own_scale = jnp.where(own_blocks >= 0, block_scale(jnp.maximum(own_blocks, 0)), 0.0)
    steps_local = precondition(own_scale, owned, root_left, root_right)
    steps_local, gain_grads = lax.optimization_barrier((steps_local, gain_grads))
    returned = lax.all_to_all(steps_local, ("dp", "wide"), split_axis=0, concat_axis=0, tiled=True)
    blocks = owned.transpose(1, 0, 2, 3).reshape(slot_dev, B, B)
    new_left = stat_decay * stat_left + (1.0 - stat_decay) * jnp.einsum(
        "nij,nkj->nik", blocks, blocks, preferred_element_type=jnp.float32
    )
    new_right = stat_decay * stat_right + (1.0 - stat_decay) * jnp.einsum(
        "nji,njk->nik", blocks, blocks, preferred_element_type=jnp.float32
    )
    new_weights = update(block_slot, returned, master_weights)
    return (
        output,
        input_grad,
        grad_local,
        new_left,
        new_right,
        new_weights,
        gain_grads,
        new_gain_moments,
        new_gains,
    )


def solution(mesh):
    placed = (
        P(("dp", "wide"), None, None),
        P(("dp", "wide"), None, None),
        P(("dp", "wide")),
        P(("dp", "wide"), None),
        P(None, ("dp", "wide")),
        P(),
        P(),
        P(),
        P(("dp", "wide"), None, None),
        P(("dp", "wide"), None, None),
        P(("dp", "wide"), None, None),
        P(("dp", "wide"), None, None),
    )
    return jax.shard_map(
        local,
        mesh=mesh,
        in_specs=placed,
        out_specs=(
            P(("dp", "wide"), None, None),
            P(("dp", "wide"), None, None),
            P(None, ("dp", "wide")),
            P(("dp", "wide"), None, None),
            P(("dp", "wide"), None, None),
            P(None, ("dp", "wide")),
            P(),
            P(),
            P(),
        ),
        check_vma=False,
    )
```

time: 3560 us -> 800 us (0.22)
  waiting for transfers between devices: 2090 us -> 48.7 us
  local copies, waits for them, and re-layouts: 1050 us -> 31.1 us
  Pallas kernels: 0 us -> 578 us
  matrix products: 219 us -> 101 us
  blocking collectives: 115 us -> 0 us
    reduce_scatter x5 -> x2, waiting for transfers between devices: 1610 us -> 0.02 us  [the longest x1 0.02 us: local(): lax.psum_scatter(down_part, 'wide', scatter_dimension=0, tiled=False)]
    pallas_call x0 -> x7, Pallas kernels: none -> 578 us  [the longest x1 261 us: gather_call(): pl.pallas_call(functools.partial(gather_kernel, line, ffn_s.shape[3] // 2...]
    unnamed x165 -> x58, local copies, waits for them, and re-layouts: 536 us -> 20.7 us
    all_gather x2 -> x1, waiting for transfers between devices: 389 us -> 0.01 us  [local(): down_all = lax.all_gather(down_s, 'wide', axis=0)]
    reshape x9 -> x1, local copies, waits for them, and re-layouts: 234 us -> 3.05 us  [local(): dot_grad(hidden, down_low).astype(low).reshape(rf, nwide, piece, D)]
    dot_general x31 -> x8, matrix products: 219 us -> 101 us  [the longest x2 33 us: dot_back(): lax.dot_general(grads, matrix, (((1,), (1,)), ((), ())), preferred_elemen...]
    psum x1 -> x0, blocking collectives: 115 us -> none  [local(): gain_grads = lax.psum(jnp.stack([gain_one, gain_two]), ('dp', 'wide'))]
    transpose x3 -> x2, local copies, waits for them, and re-layouts: 119 us -> 5.6 us  [the longest x1 3.14 us: local(): w_down = down_all.transpose(1, 0, 2, 3).reshape(rf * part, D)]
  transfers between devices with their start and end apart: 10 -> 5, of which waited for: 7 -> 1; matrix products, arithmetic and copies ran while one was open for 21% -> 12% of each run, Pallas kernels for 0% -> 70%
where the time goes in v1:
time: 800 us; the launch traced here: 792 us
  Pallas kernels  578 us (72%)
  matrix products  101 us (13%)
  waiting for transfers between devices  48.7 us (6%)
  local copies, waits for them, and re-layouts  31.1 us (4%)
  between operations  15.1 us (2%)
  other arithmetic  10.6 us (1%)
    pallas_call x1, Pallas kernels, gather_call(): pl.pallas_call(functools.partial(gather_kernel, line, ffn_s.shape[3] // 2...  261 us
    pallas_call x1, Pallas kernels, scatter_call(): pl.pallas_call(functools.partial(scatter_kernel, line, wf // 2), out_shap...  222 us
    pallas_call x1, Pallas kernels, gains_call(): pl.pallas_call(functools.partial(gains_kernel, line), out_shape=jax.Shape...  64.6 us
    all_to_all x1, waiting for transfers between devices, local(): lax.all_to_all(steps_local, ('dp', 'wide'), split_axis=0, concat_axis=0,...  48.6 us
    dot_general x2, matrix products, dot_back(): lax.dot_general(grads, matrix, (((1,), (1,)), ((), ())), preferred_elemen...  33 us
    dot_general x2, matrix products, dot(): return jnp.dot(left, right, preferred_element_type=jnp.float32)  30.1 us
    dot_general x2, matrix products, dot_grad(): lax.dot_general(rows, grads, (((0,), (0,)), ((), ())), preferred_element_...  27.8 us
    unnamed x58, local copies, waits for them, and re-layouts  20.7 us
  transfers between devices with their start and end apart: 5, of which 1 were waited for; matrix products, arithmetic and copies ran while one was open for 12% of the time, Pallas kernels for 70%

profile of v1, /device:TPU:0, one launch (start us, length us, event | category | flops | bytes accessed | tf_op | source)
XLA Modules:
  0.0 791.6 jit_solution(15587074518093777484)
XLA Ops:
  7.2 0.0 copy-start.11
  7.2 0.0 copy-start.17
  7.2 0.0 copy-start.14
  7.2 0.0 all-gather.3.cloned.1.call-start
  7.3 6.4 pack.1
  13.7 1.1 copy-done.4
  14.8 0.7 copy-done.6
  15.5 0.7 copy-done.8
  16.2 0.0 all-gather.3.cloned.1.call-update
  16.2 0.0 reduce-scatter.5.cloned.1.call-start
  17.0 0.5 multiply_cosine_fusion
  17.5 0.1 maximum_bitcast_fusion
  17.6 0.1 maximum_multiply_fusion
  17.7 0.7 pad_maximum_fusion.1.refs_5_
  18.5 0.3 fusion
  18.8 0.6 fusion.10
  19.4 1.9 fusion.2
  21.3 261.1 %gather_weights.1 = (bf16[4,4,8,16,768]{4,3,2,1,0:T(8,128)(2,1)}, bf16[4,8,16,2048]{3,2,1,0:T(8,128)(2,1)}, bf16[4,4,8,16,2816]{4,3,2,1,0:T(8,128)(2,1)}, bf16[4...) custom-call(bf16[4,4,16,768]{3,2,1,0:T(8,128)(2,1)} %copy-done.6, ...), custom_call_target="tpu_custom_call" | custom-call | tf_op jit(solution)/shard_map/gather_weights/pallas_call | solution.py:536
  282.4 19.1 %fusion.11 = f32[1024,2816]{1,0:T(8,128)} fusion(bf16[1024,2048]{1,0:T(8,128)(2,1)} %bitcast.79, bf16[2048,2816]{1,0:T(8,128)(2,1)} %bitcast.77), kind=kOutput, calls=%fused_computation.42 | convolution fusion | flops 11811160064 | bytes 27262976 | tf_op jit(solution)/shard_map/dot_general | solution.py:102
  301.5 3.1 copy.29
  304.7 0.0 copy-start.12
  304.7 16.7 %multiply_convert_fusion.1 = (bf16[1024,1408]{1,0:T(8,128)(2,1)S(1)}, bf16[1024,1408]{1,0:T(8,128)(2,1)}, bf16[1024,1408]{1,0:T(8,128)(2,1)}) fusion(f32[1024,2816]{1,0:T(8,128)} %fusion.11, bf16[1024,2048]{1,0:T(8,128)(2,1)} %bitcast.81, bf16[1408,2048]{1,0:T(8,128)(2,1)S(1)} %bitcast.66), kind=kOutput, calls=%fused_computation.8 | convolution fusion | flops 5928648704 | bytes 30146560 | tf_op jit(solution)/shard_map/dot_general | solution.py:106
  321.4 8.9 %convolution_convert_fusion.1 = bf16[1408,2048]{1,0:T(8,128)(2,1)S(1)} fusion(bf16[1024,1408]{1,0:T(8,128)(2,1)} %get-tuple-element.63, bf16[1024,2048]{1,0:T(8,128)(2,1)} %bitcast.82), kind=kOutput, calls=%fused_computation.2 | convolution fusion | flops 5908463616 | bytes 12845056 | tf_op jit(solution)/shard_map/dot_general | solution.py:112
  330.3 0.0 copy-start.15
  330.3 3.0 copy.36
  333.3 2.9 pad_maximum_fusion
  336.3 0.0 reduce-scatter.5.cloned.1.call-update
  336.3 0.7 copy-done.10
  337.0 1.1 scatter_custom_fusion.slot_ref
  338.1 0.0 copy-start.13
  338.1 18.9 %convolution_convert_fusion = bf16[2048,2816]{1,0:T(8,128)(2,1)} fusion(bf16[1024,2048]{1,0:T(8,128)(2,1)} %bitcast.80, bf16[1024,2816]{1,0:T(8,128)(2,1)} %pad_maximum_fusion), kind=kOutput, calls=%fused_computation.1 | convolution fusion | flops 11816927232 | bytes 21495808 | tf_op jit(solution)/shard_map/dot_general | solution.py:112
  357.0 16.3 %convolution_convert_fusion.2 = bf16[1024,2048]{1,0:T(8,128)(2,1)} fusion(bf16[1024,2816]{1,0:T(8,128)(2,1)S(1)} %copy-done.13, bf16[2048,2816]{1,0:T(8,128)(2,1)} %bitcast.78), kind=kOutput, calls=%fused_computation.11 | convolution fusion | flops 11813257216 | bytes 21495808 | tf_op jit(solution)/shard_map/dot_general | solution.py:106
  373.3 222.0 %scatter_grads.1 = (bf16[4,4,16,768]{3,2,1,0:T(8,128)(2,1)}, bf16[4,16,2048]{2,1,0:T(8,128)(2,1)}, bf16[4,4,16,2816]{3,2,1,0:T(8,128)(2,1)}, bf16[256,2048]{1,0:T(8,128)(2,1)}, f32[2,2048]{1,0:T(2,128)}) custom-call(bf16[4,4,4,2,16,2816]{5,4,3,2,1,0:T(8,128)(2,1)} %bitcast.60, bf16[4,256,2048]{2,1,0:T(8,128)(2,1)} %bitcast.71, ...), custom_call_target="tpu_custom_call" | custom-call | tf_op jit(solution)/shard_map/scatter_grads/pallas_call | solution.py:1077
  595.3 0.0 reduce-scatter.5.cloned.1.call-done
  595.3 1.4 copy-done.3
  596.7 1.1 copy-done.5
  597.8 1.0 copy-done.7
  598.8 0.9 copy-done.9
  599.8 3.3 to_slots.1
  603.0 1.6 copy-done.1
  604.6 3.9 all-to-all-start
  608.5 0.0 reduce-scatter.3.cloned.1.call-start
  608.6 11.0 %convolution_convert_fusion.3 = bf16[1024,2048]{1,0:T(8,128)(2,1)} fusion(bf16[1024,1408]{1,0:T(8,128)(2,1)S(1)} %copy-done.22, bf16[1408,2048]{1,0:T(8,128)(2,1)} %bitcast.67), kind=kOutput, calls=%fused_computation.12 | convolution fusion | flops 5907677184 | bytes 12845056 | tf_op jit(solution)/shard_map/dot_general | solution.py:102
  619.6 0.0 reduce-scatter.3.cloned.1.call-update
  619.6 0.1 compare_select_fusion.4.scale_ref
  619.7 64.6 %sum_gains.1 = f32[2,2048]{1,0:T(2,128)} custom-call(f32[2,2048]{1,0:T(2,128)} %get-tuple-element.56.part_ref), custom_call_target="tpu_custom_call" | custom-call | tf_op jit(solution)/shard_map/sum_gains/pallas_call | solution.py:1159
  684.3 0.0 all-to-all-done.grad_ref
  684.3 9.9 %precondition.1 = bf16[32,6,16,512]{3,2,1,0:T(8,128)(2,1)S(1)} custom-call(f32[6]{0:T(128)S(1)} %compare_select_fusion.4.scale_ref, bf16[32,6,16,512]{3,2,1,0:T(8,128)(2,1)} %all-to-all-done.grad_ref, f32[6,512,512]{2,1,0:T(8,128)} %left_ref.1, f32[6,512,512]{2,1,0:T(8,128)} %right_ref.1), custom_call_target="tpu_custom_call" | custom-call | tf_op jit(solution)/shard_map/precondition/pallas_call | solution.py:1484
  694.3 0.0 copy-start
  694.3 1.7 copy-done
  695.9 3.4 all-to-all-start.1
  699.4 0.7 fusion.6
  700.1 3.3 fusion.3
  703.4 0.8 pad.8
  704.1 0.0 slice-start.1
  704.1 7.4 copy.34
  711.6 2.5 copy.31
  714.1 0.0 slice-start.3
  714.1 4.9 multiply_add_fusion
  719.0 4.8 multiply_add_fusion.1
  723.8 48.6 %all-to-all-done.1.steps_ref = bf16[32,6,16,512]{3,2,1,0:T(8,128)(2,1)S(1)} async-done(((bf16[32,6,16,512]{3,2,1,0:T(8,128)(2,1)}), bf16[32,6,16,512]{3,2,1,0:T(8,128)(2,1)S(1)}, u32[]{:S(2)}, u32[]{:S(2)}) %all-to-all-start.1) | async-done | bytes 3145760 | tf_op jit(solution)/shard_map/all_to_all | solution.py:1708
  772.4 10.8 %update.1 = f32[172,8192]{1,0:T(8,128)} custom-call(s32[172]{0:T(256)S(1)} %copy-done.10, bf16[32,6,16,512]{3,2,1,0:T(8,128)(2,1)S(1)} %all-to-all-done.1.steps_ref, f32[172,8192]{1,0:T(8,128)} %master_ref.1), custom_call_target="tpu_custom_call" | custom-call | tf_op jit(solution)/shard_map/update/pallas_call | solution.py:1434
  783.1 1.0 copy.40
  784.1 0.6 copy.41
  (45 shorter events, 0.1 us)
Async XLA Ops:
  7.2 9.8 %copy-start.21 = (s32[1,256]{1,0:T(1,128)S(1)}, s32[1,256]{1,0:T(1,128)}, u32[]{:S(2)}) copy-start(s32[1,256]{1,0:T(1,128)} %param.15) | copy-start | bytes 3076
  7.2 11.3 %copy-start.11 = (bf16[1,256,2048]{2,1,0:T(8,128)(2,1)S(1)}, bf16[1,256,2048]{2,1,0:T(8,128)(2,1)}, u32[]{:S(2)}) copy-start(bf16[1,256,2048]{2,1,0:T(8,128)(2,1)} %param.12) | copy-start | bytes 3145732
  7.2 11.6 %copy-start.17 = (f32[2,2048]{1,0:T(2,128)S(1)}, f32[2,2048]{1,0:T(2,128)}, u32[]{:S(2)}) copy-start(f32[2,2048]{1,0:T(2,128)} %refs_12_.1) | copy-start | bytes 49156
  7.2 12.2 %copy-start.14 = (bf16[1,256,2048]{2,1,0:T(8,128)(2,1)S(1)}, bf16[1,256,2048]{2,1,0:T(8,128)(2,1)}, u32[]{:S(2)}) copy-start(bf16[1,256,2048]{2,1,0:T(8,128)(2,1)} %param.13) | copy-start | bytes 3145732
  7.2 294.3 %all-gather.3.cloned.1.call-start = ((), (), s32[]{:S(2)}) async-start(), calls=%async_computation.6 | async-start | bytes 6488064 | tf_op jit(solution)/shard_map/all_gather | solution.py:1631
  13.7 1.1 copy-start.4
  14.8 0.7 copy-start.6
  15.5 0.7 copy-start.8
  16.2 579.1 %reduce-scatter.5.cloned.1.call-start = ((), (), s32[]{:S(2)}) async-start(), calls=%async_computation.5 | async-start | bytes 6488064 | tf_op jit(solution)/shard_map/reduce_scatter | solution.py:1673
  304.7 16.7 %copy-start.12 = (bf16[11,8,16,2048]{3,2,1,0:T(8,128)(2,1)}, bf16[11,8,16,2048]{3,2,1,0:T(8,128)(2,1)S(1)}, u32[]{:S(2)}) copy-start(bf16[11,8,16,2048]{3,2,1,0:T(8,128)(2,1)S(1)} %copy.29) | copy-start | bytes 17301508
  330.3 3.1 copy-start.15
  336.3 0.7 copy-start.10
  338.1 18.9 %copy-start.13 = (bf16[1024,2816]{1,0:T(8,128)(2,1)S(1)}, bf16[1024,2816]{1,0:T(8,128)(2,1)}, u32[]{:S(2)}) copy-start(bf16[1024,2816]{1,0:T(8,128)(2,1)} %pad_maximum_fusion) | copy-start | bytes 17301508
  373.3 235.2 %copy-start.22 = (bf16[1024,1408]{1,0:T(8,128)(2,1)S(1)}, bf16[1024,1408]{1,0:T(8,128)(2,1)}, u32[]{:S(2)}) copy-start(bf16[1024,1408]{1,0:T(8,128)(2,1)} %get-tuple-element.63) | copy-start | bytes 8650756
  595.3 1.4 copy-start.3
  596.7 1.1 copy-start.5
  597.8 1.0 copy-start.7
  598.8 0.9 copy-start.9
  603.0 1.6 copy-start.1
  604.6 79.7 %all-to-all-start = ((bf16[32,6,16,512]{3,2,1,0:T(8,128)(2,1)}), bf16[32,6,16,512]{3,2,1,0:T(8,128)(2,1)}, u32[]{:S(2)}, u32[]{:S(2)}) async-start(bf16[32,6,16,512]{3,2,1,0:T(8,128)(2,1)} %get-tuple-element.55), calls=%async_computation.2 | async-start | bytes 6291456 | tf_op jit(solution)/shard_map/all_to_all | solution.py:1701
  608.5 91.5 %reduce-scatter.3.cloned.1.call-start = ((), (), s32[]{:S(2)}) async-start(), calls=%async_computation.4 | async-start | bytes 5242880 | tf_op jit(solution)/shard_map/reduce_scatter | solution.py:122
  694.3 1.7 copy-start
  695.9 3.4 copy-start.18
  695.9 3.4 copy-start.19
  695.9 3.5 copy-start.20
  695.9 76.4 %all-to-all-start.1 = ((bf16[32,6,16,512]{3,2,1,0:T(8,128)(2,1)}), bf16[32,6,16,512]{3,2,1,0:T(8,128)(2,1)S(1)}, u32[]{:S(2)}, u32[]{:S(2)}) async-start(bf16[32,6,16,512]{3,2,1,0:T(8,128)(2,1)} %copy-done), calls=%async_computation.3 | async-start | bytes 6291456 | tf_op jit(solution)/shard_map/all_to_all | solution.py:1708
  700.1 3.3 copy-start.2
  703.4 10.7 %slice-start = ((s8[6291456]{0:T(1024)(128)(4,1)}), s8[4194304]{0:T(1024)(128)(4,1)S(1)}, s32[]{:S(2)}) async-start(s8[6291456]{0:T(1024)(128)(4,1)} %bitcast.61), calls=%async_computation.7 | async-start | bytes 8388608
  704.1 9.9 %slice-start.1 = ((s8[6291456]{0:T(1024)(128)(4,1)}), s8[2097152]{0:T(1024)(128)(4,1)S(1)}, s32[]{:S(2)}) async-start(s8[6291456]{0:T(1024)(128)(4,1)} %bitcast.61), calls=%async_computation.8 | async-start | bytes 4194304
  711.6 7.4 slice-start.2
  714.1 4.9 slice-start.3
  772.4 10.8 %copy-start.16 = (bf16[256,2048]{1,0:T(8,128)(2,1)S(1)}, bf16[256,2048]{1,0:T(8,128)(2,1)}, u32[]{:S(2)}) copy-start(bf16[256,2048]{1,0:T(8,128)(2,1)} %get-tuple-element.49) | copy-start | bytes 3145732
Sparse Core Ops, SparseCore 0:
  16.4 125.5 all-gather.2
  336.4 149.9 reduce-scatter.4
  619.7 53.1 reduce-scatter.2

commit v2 on v1

--- a/solution.py
+++ b/solution.py
@@ -170,14 +170,14 @@
     lax.fori_loop(0, count, body, 0)
 
 
-def gather_kernel(line, half, *refs):
-    sent_in, (residual_ref, scale_ref, gain_ref) = refs[:6], refs[6:9]
-    outs, (qkv_out, attn_out, middle_out, normed_out) = refs[9:13], refs[13:17]
-    rows_out, tables_out = refs[17:19]
-    rows_v, tables_v, wqkv_v, wout_v, qkv_v, attn_v, part_v, sum_v, normed_v = refs[19:28]
-    loc, dp_send, dp_recv, up_sem, dn_sem, y_sem, recv, keep, sum_send, sum_recv, norm_send, norm_recv = refs[28:]
+def gather_kernel(line, blocks, half, *refs):
+    sent_in, down_s, (residual_ref, scale_ref, gain_ref) = refs[:6], refs[6], refs[7:10]
+    outs, (qkv_out, attn_out, middle_out, normed_out) = refs[10:15], refs[15:19]
+    rows_out, tables_out = refs[19:21]
+    rows_v, tables_v, wqkv_v, wout_v, qkv_v, attn_v, part_v, sum_v, normed_v = refs[21:30]
+    loc, dp_send, dp_recv, up_sem, dn_sem, y_sem, recv, keep, sum_send, sum_recv, norm_send, norm_recv = refs[30:]
     qkv_s, out_s, ffn_s = sent_in[:3]
-    qkv, out, ffn, low_out = outs
+    qkv, out, ffn, down, low_out = outs
     row_to = (rows_v, low_out, tables_v)
     f32, low = jnp.float32, jnp.bfloat16
     j, w = lax.axis_index("dp"), lax.axis_index("wide")
@@ -213,7 +213,7 @@
     ] + [
         pltpu.make_async_copy(sent_in[3 + place], row_to[place].at[j], loc.at[3 + place])
         for place in range(3)
-    ]
+    ] + [pltpu.make_async_copy(down_s, down.at[:, w], loc.at[6])]
     for copy in copies:
         copy.start()
     for place in range(2):
@@ -223,11 +223,9 @@
     chunks = []
     for part in range(4):
         chunks += [("qkv", part, 0), ("out", part, 0)]
-        if part == 0:
-            chunks += [("ffn", 0, 0)]
-    chunks += [("ffn", 0, 1)]
-    for part in range(1, 4):
+    for part in range(4):
         chunks += [("ffn", part, 0), ("ffn", part, 1)]
+    chunks += [("down", slice(0, blocks // 2), 0), ("down", slice(blocks // 2, blocks), 0)]
     count = len(chunks)
 
     def crosses_first(at):
@@ -240,6 +238,8 @@
             return qkv.at[:, flip(j, part), origin]
         if name == "out":
             return out.at[flip(j, part), origin]
+        if name == "down":
+            return down.at[part, origin]
         return ffn.at[:, flip(j, part), origin, :, side * half : (side + 1) * half]
 
     def up(at, origin):
@@ -273,8 +273,11 @@
 
     def own(at):
         name, part, side = chunks[at]
-        place = ("qkv", "out", "ffn").index(name)
-        if (place, part) not in waited:
+        place = ("qkv", "out", "ffn", "down").index(name)
+        if place == 3:
+            if part.start == 0:
+                copies[6].wait()
+        elif (place, part) not in waited:
             waited.append((place, part))
             if part == 0:
                 copies[place].wait()
@@ -437,40 +440,40 @@
             work.append(functools.partial(attend, part, head))
         work.append(functools.partial(project_out, part))
     work.append(normalize)
-    ready = attn_chunks[-1] + line + 1
+    ready = attn_chunks[-1] + line
 
     def compute(pieces):
         for _ in range(pieces):
             if work:
                 work.pop(0)()
 
-    for step in range(count + line):
+    for step in range(count + line - 1):
         if step < count:
             own(step)
         for far in range(1, line):
-            at = step - far - 1
+            at = step - far
             if 0 <= at < count:
                 if far == 1 and crosses_first(at):
                     turn(at)
                 pass_on(at, far, start, True)
                 if step >= ready:
-                    compute(2)
+                    compute(1)
         if step == 2:
             for part in range(1, 4):
                 weight_copy(part, 2).start()
-        if step == attn_chunks[-1]:
+        if step == attn_chunks[-1] - 1:
             for part in (1, 2):
                 row_copy(part, 0).start()
                 row_copy(part, 2).start()
-        if step == attn_chunks[-1] + 2:
-            for part in (1, 2):
-                row_copy(part, 1).start()
         if step == ready - 1:
             hand_on(0)
             hand_on(2)
+        if step == ready:
+            for part in (1, 2):
+                row_copy(part, 1).start()
         if step >= ready:
-            compute(2)
-        if step == count + 1:
+            compute(1)
+        if step == count:
             hand_on(1)
     compute(len(work))
     send_normed(2).wait_recv()
@@ -508,7 +511,7 @@
     keep_tables.wait()
 
 
-def gather_call(line, qkv_s, out_s, ffn_s, rows, low_rows, tables, residual, scale, gain):
+def gather_call(line, qkv_s, out_s, ffn_s, down_s, rows, low_rows, tables, residual, scale, gain):
     low = jnp.bfloat16
     ndp, wide = qkv_s.shape[0], 2 * line
     rm, piece = qkv_s.shape[1], qkv_s.shape[2]
@@ -521,6 +524,7 @@
         shape(rm, ndp, wide, piece, qkv_s.shape[3]),
         shape(ndp, wide, piece, out_s.shape[2]),
         shape(rm, ndp, wide, piece, ffn_s.shape[3]),
+        shape(down_s.shape[0], wide, piece, down_s.shape[2]),
         shape(ndp, seq, D),
         shape(ndp, seq, qkv_s.shape[3]),
         shape(ndp, seq, wq),
@@ -531,13 +535,13 @@
     )
     dma = pltpu.SemaphoreType.DMA
     whole = pl.BlockSpec(memory_space=pltpu.VMEM)
-    args = (qkv_s, out_s, ffn_s, rows, low_rows, tables)
-    count = 16
+    args = (qkv_s, out_s, ffn_s, rows, low_rows, tables, down_s)
+    count = 18
     return pl.pallas_call(
-        functools.partial(gather_kernel, line, ffn_s.shape[3] // 2),
+        functools.partial(gather_kernel, line, down_s.shape[0], ffn_s.shape[3] // 2),
         out_shape=outs,
         in_specs=[ANY] * len(args) + [whole, pl.BlockSpec(memory_space=pltpu.SMEM), whole],
-        out_specs=[ANY] * 6 + [whole] + [ANY] * 3,
+        out_specs=[ANY] * 7 + [whole] + [ANY] * 3,
         scratch_shapes=[
             pltpu.VMEM((ndp, seq, D), low),
             pltpu.VMEM((ndp, *tables.shape), tables.dtype),
@@ -1205,11 +1209,11 @@
     return exp_scores / jnp.sum(exp_scores, -1, keepdims=True)
 
 
-def gather_weights(qkv_s, out_s, ffn_s, rows, low_rows, tables, residual, scale, gain):
+def gather_weights(qkv_s, out_s, ffn_s, down_s, rows, low_rows, tables, residual, scale, gain):
     ndp, nwide = lax.axis_size("dp"), lax.axis_size("wide")
     if ndp == 4 and nwide == 8 and qkv_s.shape[2] % 16 == 0:
         return gather_call(
-            nwide // 2, qkv_s, out_s, ffn_s, rows, low_rows, tables, residual, scale, gain
+            nwide // 2, qkv_s, out_s, ffn_s, down_s, rows, low_rows, tables, residual, scale, gain
         )
 
     def spread(values):
@@ -1238,6 +1242,7 @@
         w_qkv,
         w_out,
         w_ffn,
+        lax.all_gather(down_s, "wide", axis=1),
         lax.all_gather(low_rows, "dp", axis=0),
         packed,
         out_low,
@@ -1405,27 +1410,21 @@
 
 def update_kernel(piece, slot_ref, steps_ref, master_ref, out_ref, flat_ref):
     each_slot = steps_ref.shape[1]
-    count = master_ref.shape[0]
-
-    def block(index, carry):
-        slot = slot_ref[index]
+    size = master_ref.shape[0]
+    last = slot_ref.shape[0] - 1
+    for index in range(size):
+        slot = slot_ref[jnp.minimum(pl.program_id(0) * size + index, last)]
         value = steps_ref[slot // each_slot, slot % each_slot].astype(jnp.float32)
-        rows = pl.ds(pl.multiple_of(index * piece, piece), piece)
         for group in range(B // 128):
-            flat_ref[group, rows, :] = value[:, group * 128 : (group + 1) * 128]
-        return carry
-
-    lax.fori_loop(0, count, block, 0)
-    for first in range(0, count, 8):
-        size = min(8, count - first)
-        for row in range(piece):
-            for group in range(B // 128):
-                step = flat_ref[group, pl.ds(first * piece + row, size, stride=piece), :]
-                start = row * B + group * 128
-                columns = slice(start, start + 128)
-                out_ref[first : first + size, columns] = (1.0 - weight_decay) * master_ref[
-                    first : first + size, columns
-                ] - step
+            flat_ref[group, index * piece : (index + 1) * piece, :] = value[
+                :, group * 128 : (group + 1) * 128
+            ]
+    for row in range(piece):
+        for group in range(B // 128):
+            step = flat_ref[group, pl.ds(row, size, stride=piece), :]
+            start = row * B + group * 128
+            columns = slice(start, start + 128)
+            out_ref[:, columns] = (1.0 - weight_decay) * master_ref[:, columns] - step
 
 
 def vmem_call(kernel, outs, args, scratch=(), prefetch=0, name=None):
@@ -1493,15 +1492,23 @@
 
 
 def update_call(block_slot, returned, master):
-    piece = master.shape[1] // B
-    return vmem_call(
-        functools.partial(update_kernel, piece),
-        jax.ShapeDtypeStruct(master.shape, jnp.float32),
-        (block_slot, returned, master),
-        [pltpu.VMEM((B // 128, NBLK * piece, 128), jnp.float32)],
-        prefetch=1,
+    count, width = master.shape
+    size = 16
+    rows = pl.BlockSpec((size, width), lambda step: (step, 0))
+    return pl.pallas_call(
+        functools.partial(update_kernel, width // B),
+        out_shape=jax.ShapeDtypeStruct(master.shape, jnp.float32),
+        grid=(pl.cdiv(count, size),),
+        in_specs=[
+            pl.BlockSpec(memory_space=pltpu.SMEM),
+            pl.BlockSpec(memory_space=pltpu.VMEM),
+            rows,
+        ],
+        out_specs=rows,
+        scratch_shapes=[pltpu.VMEM((B // 128, size * width // B, 128), jnp.float32)],
+        compiler_params=pltpu.CompilerParams(vmem_limit_bytes=48 * 1024 * 1024),
         name="update",
-    )
+    )(block_slot, returned, master)
 
 
 def pack(master_weights, ndp):
@@ -1628,13 +1635,13 @@
     rate_one = norm_rate(residual)
 
     qkv_s, out_s, ffn_s, down_s = pack(master_weights, ndp)
-    down_all = lax.all_gather(down_s, "wide", axis=0)
     cosine_table, sine_table = rope_tables(positions[0])
     signs = jnp.where(jnp.arange(HD) < HD // 2, -1.0, 1.0)
     (
         w_qkv,
         w_out,
         w_ffn,
+        w_down,
         down_low,
         packed,
         out_low,
@@ -1646,6 +1653,7 @@
         qkv_s,
         out_s,
         ffn_s,
+        down_s,
         (residual * rate_one * gains[0]).astype(low),
         (branch_scale * out_grad_f).astype(low),
         jnp.stack([cosine_table, sine_table * signs]),
@@ -1654,7 +1662,7 @@
         gains[1:],
     )
     w_ffn = w_ffn.reshape(D, 2 * rf * part)
-    w_down = down_all.transpose(1, 0, 2, 3).reshape(rf * part, D)
+    w_down = w_down.reshape(rf * part, D)
     normed_two = normed_two.reshape(tokens, D)
     down_low = down_low.reshape(tokens, D)
 
@@ -1668,9 +1676,9 @@
     ).astype(low)
     up_low = (hidden_grad * gate_rows * sigmoid_gate).astype(low)
     ffn_low = jnp.concatenate([gate_low, up_low], 1)
-    down_part = dot_grad(hidden, down_low).astype(low).reshape(rf, nwide, piece, D)
-    down_part, ffn_low = lax.optimization_barrier((down_part.transpose(1, 0, 2, 3), ffn_low))
-    grad_down = lax.psum_scatter(down_part, "wide", scatter_dimension=0, tiled=False)
+    down_part = dot_grad(hidden, down_low).astype(low).reshape(rf, nwide * piece, D)
+    down_part, w_ffn, normed_two = lax.optimization_barrier((down_part, w_ffn, normed_two))
+    grad_down = lax.psum_scatter(down_part, "wide", scatter_dimension=1, tiled=True)
     result = middle + branch_scale * total(dot(hidden, w_down))
     output = result.astype(low)[None]
     grad_qkv, grad_out, grad_ffn, input_grad, gain_parts = scatter_grads(

time: 800 us -> 792 us (0.990)
    pallas_call x3 -> x2, Pallas kernels: 20.4 us -> 8.67 us  [vmem_call(): pl.pallas_call(kernel, out_shape=outs, in_specs=[small] * prefetch + [who...]
    pallas_call x1 -> x2, Pallas kernels: 261 us -> 270 us  [the longest x1 260 us: gather_call(): pl.pallas_call(functools.partial(gather_kernel, line, down_s.shape[0], ff...]
    unnamed x58 -> x60, local copies, waits for them, and re-layouts: 20.7 us -> 21.6 us
  transfers between devices with their start and end apart: 5 -> 4, of which waited for: 1 -> 1; matrix products, arithmetic and copies ran while one was open for 12% -> 9% of each run, Pallas kernels for 70% -> 38%
where the time goes in v2:
time: 792 us; the launch traced here: 783 us
  Pallas kernels  576 us (73%)
  matrix products  97.8 us (12%)
  waiting for transfers between devices  48.6 us (6%)
  local copies, waits for them, and re-layouts  26.6 us (3%)
  between operations  17 us (2%)
  other arithmetic  8.89 us (1%)
    pallas_call x1, Pallas kernels, gather_call(): pl.pallas_call(functools.partial(gather_kernel, line, down_s.shape[0], ff...  260 us
    pallas_call x1, Pallas kernels, scatter_call(): pl.pallas_call(functools.partial(scatter_kernel, line, wf // 2), out_shap...  223 us
    pallas_call x1, Pallas kernels, gains_call(): pl.pallas_call(functools.partial(gains_kernel, line), out_shape=jax.Shape...  64.7 us
    all_to_all x1, waiting for transfers between devices, local(): lax.all_to_all(steps_local, ('dp', 'wide'), split_axis=0, concat_axis=0,...  48.5 us
    dot_general x2, matrix products, dot(): return jnp.dot(left, right, preferred_element_type=jnp.float32)  30.3 us
    dot_general x2, matrix products, dot_back(): lax.dot_general(grads, matrix, (((1,), (1,)), ((), ())), preferred_elemen...  29.9 us
    dot_general x2, matrix products, dot_grad(): lax.dot_general(rows, grads, (((0,), (0,)), ((), ())), preferred_element_...  27.9 us
    unnamed x60, local copies, waits for them, and re-layouts  21.6 us
  transfers between devices with their start and end apart: 4, of which 1 were waited for; matrix products, arithmetic and copies ran while one was open for 9% of the time, Pallas kernels for 38%

profile of v2, /device:TPU:0, one launch (start us, length us, event | category | flops | bytes accessed | tf_op | source)
XLA Modules:
  0.0 782.6 jit_solution(14796406099690366559)
XLA Ops:
  8.0 0.0 copy-start.12
  8.0 0.0 copy-start.18
  8.0 0.0 copy-start.13
  8.0 0.0 reduce-scatter.5.cloned.1.call-start
  8.9 1.4 fusion.12
  10.3 1.5 fusion
  11.8 5.4 pack.1
  17.2 0.0 copy-start.4
  17.2 1.1 copy-done.4
  18.3 0.9 copy-done.5
  19.2 0.7 copy-done.7
  19.9 0.7 copy-done.9
  20.6 0.5 multiply_cosine_fusion
  21.2 0.1 maximum_bitcast_fusion
  21.3 0.1 maximum_multiply_fusion
  21.4 0.7 pad_maximum_fusion.3.refs_5_
  22.1 1.9 fusion.2
  24.0 260.1 %gather_weights.1 = (bf16[4,4,8,16,768]{4,3,2,1,0:T(8,128)(2,1)}, bf16[4,8,16,2048]{3,2,1,0:T(8,128)(2,1)}, bf16[4,4,8,16,2816]{4,3,2,1,0:T(8,128)(2,1)}, bf16[1...) custom-call(bf16[4,4,16,768]{3,2,1,0:T(8,128)(2,1)} %copy-done.7, ...), custom_call_target="tpu_custom_call" | custom-call | tf_op jit(solution)/shard_map/gather_weights/pallas_call | solution.py:540
  284.1 19.3 %fusion.13 = f32[1024,2816]{1,0:T(8,128)} fusion(bf16[1024,2048]{1,0:T(8,128)(2,1)} %bitcast.67, bf16[2048,2816]{1,0:T(8,128)(2,1)} %bitcast.63), kind=kOutput, calls=%fused_computation.43 | convolution fusion | flops 11811160064 | bytes 27262976 | tf_op jit(solution)/shard_map/dot_general | solution.py:102
  303.4 13.6 %multiply_convert_fusion.1 = (bf16[1024,1408]{1,0:T(8,128)(2,1)}, bf16[1024,1408]{1,0:T(8,128)(2,1)}, bf16[1024,1408]{1,0:T(8,128)(2,1)}) fusion(f32[1024,2816]{1,0:T(8,128)} %fusion.13, bf16[1024,2048]{1,0:T(8,128)(2,1)S(1)} %bitcast.69, bf16[1408,2048]{1,0:T(8,128)(2,1)S(1)} %bitcast.66), kind=kOutput, calls=%fused_computation.7 | convolution fusion | flops 5928648704 | bytes 30146560 | tf_op jit(solution)/shard_map/dot_general | solution.py:106
  317.0 9.8 %convolution_convert_fusion.1 = bf16[1408,2048]{1,0:T(8,128)(2,1)} fusion(bf16[1024,1408]{1,0:T(8,128)(2,1)} %get-tuple-element.67, bf16[1024,2048]{1,0:T(8,128)(2,1)S(1)} %bitcast.70), kind=kOutput, calls=%fused_computation.2 | convolution fusion | flops 5908463616 | bytes 12845056 | tf_op jit(solution)/shard_map/dot_general | solution.py:112
  326.8 0.0 reduce-scatter.5.cloned.1.call-update
  326.9 0.7 copy-done.11
  327.5 1.1 scatter_custom_fusion.slot_ref
  328.6 0.0 copy-done.22
  328.7 0.0 copy-start.23
  328.7 18.1 %convolution_convert_fusion = bf16[2048,2816]{1,0:T(8,128)(2,1)} fusion(bf16[1024,2048]{1,0:T(8,128)(2,1)} %bitcast.68, bf16[1024,1408]{1,0:T(8,128)(2,1)} %get-tuple-element.66, bf16[1024,1408]{1,0:T(8,128)(2,1)S(1)} %copy-done.22), kind=kOutput, calls=%fused_computation.1 | convolution fusion | flops 11828461568 | bytes 21495808 | tf_op jit(solution)/shard_map/dot_general | solution.py:112
  346.8 0.0 copy-done.23
  346.8 16.3 %convolution_convert_fusion.2 = bf16[1024,2048]{1,0:T(8,128)(2,1)} fusion(bf16[2048,2816]{1,0:T(8,128)(2,1)} %bitcast.64, bf16[1024,1408]{1,0:T(8,128)(2,1)S(1)} %copy-done.23, bf16[1024,1408]{1,0:T(8,128)(2,1)S(1)} %copy-done.22), kind=kOutput, calls=%fused_computation.10 | convolution fusion | flops 11824791552 | bytes 21495808 | tf_op jit(solution)/shard_map/dot_general | solution.py:106
  363.1 222.7 %scatter_grads.1 = (bf16[4,4,16,768]{3,2,1,0:T(8,128)(2,1)}, bf16[4,16,2048]{2,1,0:T(8,128)(2,1)}, bf16[4,4,16,2816]{3,2,1,0:T(8,128)(2,1)}, bf16[256,2048]{1,0:T(8,128)(2,1)}, f32[2,2048]{1,0:T(2,128)}) custom-call(bf16[4,4,4,2,16,2816]{5,4,3,2,1,0:T(8,128)(2,1)} %bitcast.49, bf16[4,256,2048]{2,1,0:T(8,128)(2,1)} %bitcast.57, ...), custom_call_target="tpu_custom_call" | custom-call | tf_op jit(solution)/shard_map/scatter_grads/pallas_call | solution.py:1081
  585.8 0.0 reduce-scatter.5.cloned.1.call-done.refs_3_
  585.9 1.4 copy-done.3
  587.2 1.1 copy-done.6
  588.3 1.0 copy-done.8
  589.3 0.9 copy-done.10
  590.3 3.3 to_slots.1
  593.5 1.6 copy-done.1
  595.1 3.9 all-to-all-start
  599.0 0.0 reduce-scatter.3.cloned.1.call-start
  599.1 11.0 %convolution_convert_fusion.3 = bf16[1024,2048]{1,0:T(8,128)(2,1)} fusion(bf16[1024,1408]{1,0:T(8,128)(2,1)S(1)} %copy-done.21, bf16[1408,2048]{1,0:T(8,128)(2,1)} %bitcast.65), kind=kOutput, calls=%fused_computation.11 | convolution fusion | flops 5907677184 | bytes 12845056 | tf_op jit(solution)/shard_map/dot_general | solution.py:102
  610.0 0.0 reduce-scatter.3.cloned.1.call-update
  610.1 64.7 %sum_gains.1 = f32[2,2048]{1,0:T(2,128)} custom-call(f32[2,2048]{1,0:T(2,128)} %get-tuple-element.60.part_ref), custom_call_target="tpu_custom_call" | custom-call | tf_op jit(solution)/shard_map/sum_gains/pallas_call | solution.py:1163
  674.8 0.1 compare_select_fusion.4.scale_ref
  674.9 0.0 all-to-all-done.grad_ref
  674.9 9.9 %precondition.1 = bf16[32,6,16,512]{3,2,1,0:T(8,128)(2,1)S(1)} custom-call(f32[6]{0:T(128)S(1)} %compare_select_fusion.4.scale_ref, bf16[32,6,16,512]{3,2,1,0:T(8,128)(2,1)} %all-to-all-done.grad_ref, f32[6,512,512]{2,1,0:T(8,128)} %left_ref.1, f32[6,512,512]{2,1,0:T(8,128)} %right_ref.1), custom_call_target="tpu_custom_call" | custom-call | tf_op jit(solution)/shard_map/precondition/pallas_call | solution.py:1483
  684.8 1.7 copy-done
  686.5 3.4 all-to-all-start.1
  690.0 0.0 copy-done.15
  690.0 0.0 copy-done.16
  690.0 0.0 copy-done.17
  690.0 0.7 fusion.6
  690.6 3.3 fusion.3
  693.9 0.8 pad.8
  694.7 0.0 slice-start.1
  694.7 7.4 copy.25
  702.2 2.5 copy.22
  704.7 0.0 slice-start.3
  704.7 5.0 multiply_add_fusion
  709.6 0.0 slice-done.2
  709.6 4.8 multiply_add_fusion.1
  714.4 48.5 %all-to-all-done.1.steps_ref = bf16[32,6,16,512]{3,2,1,0:T(8,128)(2,1)S(1)} async-done(((bf16[32,6,16,512]{3,2,1,0:T(8,128)(2,1)}), bf16[32,6,16,512]{3,2,1,0:T(8,128)(2,1)S(1)}, u32[]{:S(2)}, u32[]{:S(2)}) %all-to-all-start.1) | async-done | bytes 3145760 | tf_op jit(solution)/shard_map/all_to_all | solution.py:1716
  763.0 10.2 %update.1 = f32[172,8192]{1,0:T(8,128)} custom-call(s32[172]{0:T(256)S(1)} %copy-done.11, bf16[32,6,16,512]{3,2,1,0:T(8,128)(2,1)S(1)} %all-to-all-done.1.steps_ref, f32[172,8192]{1,0:T(8,128)} %master_ref.1), custom_call_target="tpu_custom_call" | custom-call | tf_op jit(solution)/shard_map/update/pallas_call | solution.py:1498
  773.2 1.0 copy.29
  774.1 0.6 copy.30
  (41 shorter events, 0.1 us)
Async XLA Ops:
  8.0 14.1 %copy-start.12 = (bf16[1,256,2048]{2,1,0:T(8,128)(2,1)S(1)}, bf16[1,256,2048]{2,1,0:T(8,128)(2,1)}, u32[]{:S(2)}) copy-start(bf16[1,256,2048]{2,1,0:T(8,128)(2,1)} %param.12) | copy-start | bytes 3145732
  8.0 12.6 %copy-start.18 = (s32[1,256]{1,0:T(1,128)S(1)}, s32[1,256]{1,0:T(1,128)}, u32[]{:S(2)}) copy-start(s32[1,256]{1,0:T(1,128)} %param.15) | copy-start | bytes 3076
  8.0 14.1 %copy-start.13 = (bf16[1,256,2048]{2,1,0:T(8,128)(2,1)S(1)}, bf16[1,256,2048]{2,1,0:T(8,128)(2,1)}, u32[]{:S(2)}) copy-start(bf16[1,256,2048]{2,1,0:T(8,128)(2,1)} %param.13) | copy-start | bytes 3145732
  8.0 577.8 %reduce-scatter.5.cloned.1.call-start = ((), (), s32[]{:S(2)}) async-start(), calls=%async_computation.5 | async-start | bytes 6488064 | tf_op jit(solution)/shard_map/reduce_scatter | solution.py:1681
  17.2 1.1 copy-start.4
  18.3 0.9 copy-start.5
  19.2 0.7 copy-start.7
  19.9 0.7 copy-start.9
  284.1 19.3 %copy-start.19 = (bf16[11,8,16,2048]{3,2,1,0:T(8,128)(2,1)S(1)}, bf16[11,8,16,2048]{3,2,1,0:T(8,128)(2,1)}, u32[]{:S(2)}) copy-start(bf16[11,8,16,2048]{3,2,1,0:T(8,128)(2,1)} %get-tuple-element.43) | copy-start | bytes 17301508
  284.1 19.3 %copy-start.20 = (bf16[4,256,2048]{2,1,0:T(8,128)(2,1)S(1)}, bf16[4,256,2048]{2,1,0:T(8,128)(2,1)}, u32[]{:S(2)}) copy-start(bf16[4,256,2048]{2,1,0:T(8,128)(2,1)} %get-tuple-element.44) | copy-start | bytes 12582916
  326.8 0.7 copy-start.11
  326.8 1.8 copy-start.22
  328.7 18.1 %copy-start.23 = (bf16[1024,1408]{1,0:T(8,128)(2,1)S(1)}, bf16[1024,1408]{1,0:T(8,128)(2,1)}, u32[]{:S(2)}) copy-start(bf16[1024,1408]{1,0:T(8,128)(2,1)} %get-tuple-element.66) | copy-start | bytes 8650756
  363.1 236.0 %copy-start.21 = (bf16[1024,1408]{1,0:T(8,128)(2,1)S(1)}, bf16[1024,1408]{1,0:T(8,128)(2,1)}, u32[]{:S(2)}) copy-start(bf16[1024,1408]{1,0:T(8,128)(2,1)} %get-tuple-element.67) | copy-start | bytes 8650756
  585.8 1.4 copy-start.3
  587.2 1.1 copy-start.6
  588.3 1.0 copy-start.8
  589.3 0.9 copy-start.10
  593.5 1.6 copy-start.1
  595.1 79.8 %all-to-all-start = ((bf16[32,6,16,512]{3,2,1,0:T(8,128)(2,1)}), bf16[32,6,16,512]{3,2,1,0:T(8,128)(2,1)}, u32[]{:S(2)}, u32[]{:S(2)}) async-start(bf16[32,6,16,512]{3,2,1,0:T(8,128)(2,1)} %get-tuple-element.59), calls=%async_computation.2 | async-start | bytes 6291456 | tf_op jit(solution)/shard_map/all_to_all | solution.py:1709
  599.0 91.6 %reduce-scatter.3.cloned.1.call-start = ((), (), s32[]{:S(2)}) async-start(), calls=%async_computation.4 | async-start | bytes 5242880 | tf_op jit(solution)/shard_map/reduce_scatter | solution.py:122
  684.8 1.7 copy-start
  686.5 3.4 copy-start.15
  686.5 3.4 copy-start.16
  686.5 3.5 copy-start.17
  686.5 76.4 %all-to-all-start.1 = ((bf16[32,6,16,512]{3,2,1,0:T(8,128)(2,1)}), bf16[32,6,16,512]{3,2,1,0:T(8,128)(2,1)S(1)}, u32[]{:S(2)}, u32[]{:S(2)}) async-start(bf16[32,6,16,512]{3,2,1,0:T(8,128)(2,1)} %copy-done), calls=%async_computation.3 | async-start | bytes 6291456 | tf_op jit(solution)/shard_map/all_to_all | solution.py:1716
  690.6 3.3 copy-start.2
  693.9 10.7 %slice-start = ((s8[6291456]{0:T(1024)(128)(4,1)}), s8[4194304]{0:T(1024)(128)(4,1)S(1)}, s32[]{:S(2)}) async-start(s8[6291456]{0:T(1024)(128)(4,1)} %bitcast.50), calls=%async_computation.6 | async-start | bytes 8388608
  694.7 9.9 %slice-start.1 = ((s8[6291456]{0:T(1024)(128)(4,1)}), s8[2097152]{0:T(1024)(128)(4,1)S(1)}, s32[]{:S(2)}) async-start(s8[6291456]{0:T(1024)(128)(4,1)} %bitcast.50), calls=%async_computation.7 | async-start | bytes 4194304
  702.2 7.5 slice-start.2
  704.7 5.0 slice-start.3
  763.0 10.2 %copy-start.14 = (bf16[256,2048]{1,0:T(8,128)(2,1)S(1)}, bf16[256,2048]{1,0:T(8,128)(2,1)}, u32[]{:S(2)}) copy-start(bf16[256,2048]{1,0:T(8,128)(2,1)} %get-tuple-element.53) | copy-start | bytes 3145732
Sparse Core Ops, SparseCore 0:
  327.0 151.5 reduce-scatter.4
Sparse Core Ops, SparseCore 1:
  610.2 53.0 reduce-scatter.2

commit v3 on v2

--- a/solution.py
+++ b/solution.py
@@ -1428,15 +1428,18 @@
 
 
 def vmem_call(kernel, outs, args, scratch=(), prefetch=0, name=None):
-    whole = pl.BlockSpec(memory_space=pltpu.VMEM)
+    def whole(array):
+        return pl.BlockSpec(array.shape, lambda step: (0,) * len(array.shape))
+
     small = pl.BlockSpec(memory_space=pltpu.SMEM)
     return pl.pallas_call(
         kernel,
-        out_shape=outs,
-        in_specs=[small] * prefetch + [whole] * (len(args) - prefetch),
-        out_specs=jax.tree.map(lambda _: whole, outs),
+        out_shape=[pltpu.HBM(out.shape, out.dtype) for out in outs],
+        grid=(1,),
+        in_specs=[small] * prefetch + [whole(arg) for arg in args[prefetch:]],
+        out_specs=[whole(out) for out in outs],
         scratch_shapes=list(scratch),
-        compiler_params=pltpu.CompilerParams(vmem_limit_bytes=48 * 1024 * 1024),
+        compiler_params=pltpu.CompilerParams(vmem_limit_bytes=60 * 1024 * 1024),
         name=name,
     )(*args)
 
@@ -1482,7 +1485,7 @@
     square = pl.BlockSpec((1, B, B), lambda n: (n, 0, 0))
     return pl.pallas_call(
         precondition_kernel,
-        out_shape=jax.ShapeDtypeStruct(owned.shape, jnp.bfloat16),
+        out_shape=pltpu.HBM(owned.shape, jnp.bfloat16),
         grid=(slots,),
         in_specs=[pl.BlockSpec(memory_space=pltpu.SMEM), block, square, square],
         out_specs=block,
@@ -1670,15 +1673,15 @@
     gate_rows, up_rows = ffn_rows[:, : rf * part], ffn_rows[:, rf * part :]
     sigmoid_gate = jax.nn.sigmoid(gate_rows)
     hidden = (gate_rows * sigmoid_gate * up_rows).astype(low)
-    hidden_grad = dot_back(down_low, w_down)
+    down_part = dot_grad(hidden, down_low).astype(low).reshape(rf, nwide * piece, D)
+    down_part, w_down_back = lax.optimization_barrier((down_part, w_down))
+    grad_down = lax.psum_scatter(down_part, "wide", scatter_dimension=1, tiled=True)
+    hidden_grad = dot_back(down_low, w_down_back)
     gate_low = (
         hidden_grad * up_rows * sigmoid_gate * (1.0 + gate_rows * (1.0 - sigmoid_gate))
     ).astype(low)
     up_low = (hidden_grad * gate_rows * sigmoid_gate).astype(low)
     ffn_low = jnp.concatenate([gate_low, up_low], 1)
-    down_part = dot_grad(hidden, down_low).astype(low).reshape(rf, nwide * piece, D)
-    down_part, w_ffn, normed_two = lax.optimization_barrier((down_part, w_ffn, normed_two))
-    grad_down = lax.psum_scatter(down_part, "wide", scatter_dimension=1, tiled=True)
     result = middle + branch_scale * total(dot(hidden, w_down))
     output = result.astype(low)[None]
     grad_qkv, grad_out, grad_ffn, input_grad, gain_parts = scatter_grads(

time: 792 us -> 779 us (0.984)
  local copies, waits for them, and re-layouts: 26.6 us -> 18.4 us
    unnamed x60 -> x42, local copies, waits for them, and re-layouts: 21.6 us -> 15.6 us
  transfers between devices with their start and end apart: 4 -> 4, of which waited for: 1 -> 1; matrix products, arithmetic and copies ran while one was open for 9% -> 11% of each run, Pallas kernels for 38% -> 38%
where the time goes in v3:
time: 779 us; the launch traced here: 771 us
  Pallas kernels  575 us (74%)
  matrix products  92.3 us (12%)
  waiting for transfers between devices  50.5 us (6%)
  local copies, waits for them, and re-layouts  18.4 us (2%)
  between operations  16.9 us (2%)
  other arithmetic  9.6 us (1%)
  starting transfers between devices  7.87 us (1%)
    pallas_call x1, Pallas kernels, gather_call(): pl.pallas_call(functools.partial(gather_kernel, line, down_s.shape[0], ff...  260 us
    pallas_call x1, Pallas kernels, scatter_call(): pl.pallas_call(functools.partial(scatter_kernel, line, wf // 2), out_shap...  216 us
    pallas_call x1, Pallas kernels, gains_call(): pl.pallas_call(functools.partial(gains_kernel, line), out_shape=jax.Shape...  64.9 us
    all_to_all x1, waiting for transfers between devices, local(): lax.all_to_all(steps_local, ('dp', 'wide'), split_axis=0, concat_axis=0,...  50.4 us
    dot_general x2, matrix products, dot_back(): lax.dot_general(grads, matrix, (((1,), (1,)), ((), ())), preferred_elemen...  31.2 us
    dot_general x2, matrix products, dot(): return jnp.dot(left, right, preferred_element_type=jnp.float32)  28 us
    dot_general x2, matrix products, dot_grad(): lax.dot_general(rows, grads, (((0,), (0,)), ((), ())), preferred_element_...  23.2 us
    unnamed x42, local copies, waits for them, and re-layouts  15.6 us
  transfers between devices with their start and end apart: 4, of which 1 were waited for; matrix products, arithmetic and copies ran while one was open for 11% of the time, Pallas kernels for 38%

profile of v3, /device:TPU:0, one launch (start us, length us, event | category | flops | bytes accessed | tf_op | source)
XLA Modules:
  0.0 770.5 jit_solution(3274852494257063661)
XLA Ops:
  8.0 0.0 copy-start.7
  8.0 0.0 copy-start.1
  8.0 0.0 copy-start.12
  8.0 0.0 copy-start.3
  8.1 0.0 reduce-scatter.5.cloned.1.call-start
  8.1 6.8 pack.1
  15.0 0.0 copy-done.7
  15.0 0.6 fusion.12
  15.6 0.0 copy-done.1
  15.6 0.3 fusion
  16.5 0.0 copy-done.12
  16.5 0.5 multiply_cosine_fusion
  17.1 0.1 maximum_bitcast_fusion
  17.2 0.1 maximum_multiply_fusion
  17.3 0.7 pad_maximum_fusion.3.refs_5_
  18.0 0.0 copy-done.3
  18.0 2.0 fusion.2
  20.0 260.1 %gather_weights.1 = (bf16[4,4,8,16,768]{4,3,2,1,0:T(8,128)(2,1)}, bf16[4,8,16,2048]{3,2,1,0:T(8,128)(2,1)}, bf16[4,4,8,16,2816]{4,3,2,1,0:T(8,128)(2,1)}, bf16[1...) custom-call(bf16[4,4,16,768]{3,2,1,0:T(8,128)(2,1)} %get-tuple-eleme, ...), custom_call_target="tpu_custom_call" | custom-call | tf_op jit(solution)/shard_map/gather_weights/pallas_call | solution.py:540
  280.1 17.2 %fusion.13 = f32[1024,2816]{1,0:T(8,128)S(1)} fusion(bf16[1024,2048]{1,0:T(8,128)(2,1)} %bitcast.68, bf16[2048,2816]{1,0:T(8,128)(2,1)} %bitcast.64), kind=kOutput, calls=%fused_computation.43 | convolution fusion | flops 11811160064 | bytes 27262976 | tf_op jit(solution)/shard_map/dot_general | solution.py:102
  297.3 0.0 copy-start.2
  297.3 0.0 copy-start.14
  297.3 1.8 multiply_convert_fusion.2
  299.2 3.5 copy-done.2
  302.7 1.6 copy-done.4
  304.2 0.0 copy-done.14
  304.2 8.0 %convolution_convert_fusion.1 = bf16[1408,2048]{1,0:T(8,128)(2,1)} fusion(bf16[1024,1408]{1,0:T(8,128)(2,1)S(1)} %multiply_convert_fusion.2, bf16[1024,2048]{1,0:T(8,128)(2,1)S(1)} %bitcast.71), kind=kOutput, calls=%fused_computation.2 | convolution fusion | flops 5908463616 | bytes 12845056 | tf_op jit(solution)/shard_map/dot_general | solution.py:112
  312.3 0.0 reduce-scatter.5.cloned.1.call-update
  312.3 0.7 copy-done
  312.9 1.8 scatter_custom_fusion.slot_ref
  314.8 14.7 %multiply_convert_fusion.1 = (bf16[1024,1408]{1,0:T(8,128)(2,1)S(1)}, bf16[1024,1408]{1,0:T(8,128)(2,1)S(1)}) fusion(f32[1024,2816]{1,0:T(8,128)} %copy-done.2, bf16[1024,2048]{1,0:T(8,128)(2,1)} %bitcast.70, bf16[1408,2048]{1,0:T(8,128)(2,1)} %bitcast.66), kind=kOutput, calls=%fused_computation.7 | convolution fusion | flops 5924323328 | bytes 27262976 | tf_op jit(solution)/shard_map/dot_general | solution.py:106
  329.5 0.0 copy-done.13
  329.6 15.2 %convolution_convert_fusion = bf16[2048,2816]{1,0:T(8,128)(2,1)} fusion(bf16[1024,2048]{1,0:T(8,128)(2,1)S(1)} %bitcast.69, bf16[1024,1408]{1,0:T(8,128)(2,1)S(1)} %get-tuple-element.64, bf16[1024,1408]{1,0:T(8,128)(2,1)S(1)} %get-tuple-element.63), kind=kOutput, calls=%fused_computation.1 | convolution fusion | flops 11828461568 | bytes 21495808 | tf_op jit(solution)/shard_map/dot_general | solution.py:112
  344.8 16.4 %convolution_convert_fusion.2 = bf16[1024,2048]{1,0:T(8,128)(2,1)} fusion(bf16[2048,2816]{1,0:T(8,128)(2,1)} %bitcast.65, bf16[1024,1408]{1,0:T(8,128)(2,1)S(1)} %get-tuple-element.64, bf16[1024,1408]{1,0:T(8,128)(2,1)S(1)} %get-tuple-element.63), kind=kOutput, calls=%fused_computation.10 | convolution fusion | flops 11824791552 | bytes 21495808 | tf_op jit(solution)/shard_map/dot_general | solution.py:106
  361.2 215.9 %scatter_grads.1 = (bf16[4,4,16,768]{3,2,1,0:T(8,128)(2,1)}, bf16[4,16,2048]{2,1,0:T(8,128)(2,1)}, bf16[4,4,16,2816]{3,2,1,0:T(8,128)(2,1)}, bf16[256,2048]{1,0:T(8,128)(2,1)}, f32[2,2048]{1,0:T(2,128)}) custom-call(bf16[4,4,4,2,16,2816]{5,4,3,2,1,0:T(8,128)(2,1)} %bitcast.50, bf16[4,256,2048]{2,1,0:T(8,128)(2,1)} %bitcast.58, ...), custom_call_target="tpu_custom_call" | custom-call | tf_op jit(solution)/shard_map/scatter_grads/pallas_call | solution.py:1081
  577.1 0.0 reduce-scatter.5.cloned.1.call-done.refs_3_
  577.2 5.4 to_slots.1
  582.5 3.9 all-to-all-start
  586.4 0.0 copy-start.11
  586.5 0.0 reduce-scatter.3.cloned.1.call-start
  586.5 10.9 %convolution_convert_fusion.3 = bf16[1024,2048]{1,0:T(8,128)(2,1)} fusion(bf16[1024,1408]{1,0:T(8,128)(2,1)} %copy-done.4, bf16[1408,2048]{1,0:T(8,128)(2,1)} %bitcast.67), kind=kOutput, calls=%fused_computation.11 | convolution fusion | flops 5907677184 | bytes 12845056 | tf_op jit(solution)/shard_map/dot_general | solution.py:102
  597.4 0.0 reduce-scatter.3.cloned.1.call-update
  597.4 64.9 %sum_gains.1 = f32[2,2048]{1,0:T(2,128)} custom-call(f32[2,2048]{1,0:T(2,128)} %get-tuple-element.58.part_ref), custom_call_target="tpu_custom_call" | custom-call | tf_op jit(solution)/shard_map/sum_gains/pallas_call | solution.py:1163
  662.3 0.0 copy-done.11
  662.3 0.1 compare_select_fusion.4.scale_ref
  662.4 0.0 all-to-all-done.grad_ref
  662.4 10.6 %precondition.1 = bf16[32,6,16,512]{3,2,1,0:T(8,128)(2,1)} custom-call(f32[6]{0:T(128)S(1)} %compare_select_fusion.4.scale_ref, bf16[32,6,16,512]{3,2,1,0:T(8,128)(2,1)S(1)} %all-to-all-done.grad_ref, f32[6,512,512]{2,1,0:T(8,128)} %left_ref.1, f32[6,512,512]{2,1,0:T(8,128)} %right_ref.1), custom_call_target="tpu_custom_call" | custom-call | tf_op jit(solution)/shard_map/precondition/pallas_call | solution.py:1486
  673.0 3.9 all-to-all-start.1
  676.9 0.0 copy-done.8
  676.9 0.0 copy-done.9
  676.9 0.0 copy-done.10
  676.9 0.7 fusion.6
  677.6 3.3 fusion.3
  680.9 0.8 pad.8
  681.7 0.0 slice-start.1
  681.7 7.4 copy.25
  689.1 0.4 copy.22
  689.6 0.0 slice-start.3
  689.6 5.0 multiply_add_fusion
  694.6 4.8 multiply_add_fusion.1
  699.4 50.4 %all-to-all-done.1.steps_ref = bf16[32,6,16,512]{3,2,1,0:T(8,128)(2,1)} async-done(((bf16[32,6,16,512]{3,2,1,0:T(8,128)(2,1)}), bf16[32,6,16,512]{3,2,1,0:T(8,128)(2,1)}, u32[]{:S(2)}, u32[]{:S(2)}) %all-to-all-start.1) | async-done | bytes 3145760 | tf_op jit(solution)/shard_map/all_to_all | solution.py:1719
  749.9 11.2 %update.1 = f32[172,8192]{1,0:T(8,128)} custom-call(s32[172]{0:T(256)S(1)} %copy-done, bf16[32,6,16,512]{3,2,1,0:T(8,128)(2,1)} %all-to-all-done.1.steps_ref, f32[172,8192]{1,0:T(8,128)} %master_ref.1), custom_call_target="tpu_custom_call" | custom-call | tf_op jit(solution)/shard_map/update/pallas_call | solution.py:1501
  761.1 0.0 copy-done.6
  761.1 1.0 copy.29
  762.1 0.6 copy.30
  (24 shorter events, 0.1 us)
Async XLA Ops:
  8.0 7.0 copy-start.7
  8.0 7.6 copy-start.1
  8.0 8.5 %copy-start.12 = (s32[1,256]{1,0:T(1,128)S(1)}, s32[1,256]{1,0:T(1,128)}, u32[]{:S(2)}) copy-start(s32[1,256]{1,0:T(1,128)} %param.15) | copy-start | bytes 3076
  8.0 10.0 %copy-start.3 = (bf16[1,256,2048]{2,1,0:T(8,128)(2,1)S(1)}, bf16[1,256,2048]{2,1,0:T(8,128)(2,1)}, u32[]{:S(2)}) copy-start(bf16[1,256,2048]{2,1,0:T(8,128)(2,1)} %param.13) | copy-start | bytes 3145732
  8.1 569.1 %reduce-scatter.5.cloned.1.call-start = ((), (), s32[]{:S(2)}) async-start(), calls=%async_computation.5 | async-start | bytes 6488064 | tf_op jit(solution)/shard_map/reduce_scatter | solution.py:1678
  297.3 5.3 copy-start.2
  297.3 6.9 copy-start.14
  302.7 1.6 copy-start.4
  312.3 0.7 copy-start
  314.8 14.8 %copy-start.13 = (bf16[4,256,2048]{2,1,0:T(8,128)(2,1)S(1)}, bf16[4,256,2048]{2,1,0:T(8,128)(2,1)}, u32[]{:S(2)}) copy-start(bf16[4,256,2048]{2,1,0:T(8,128)(2,1)} %get-tuple-element.40) | copy-start | bytes 12582916
  582.5 79.9 %all-to-all-start = ((bf16[32,6,16,512]{3,2,1,0:T(8,128)(2,1)}), bf16[32,6,16,512]{3,2,1,0:T(8,128)(2,1)S(1)}, u32[]{:S(2)}, u32[]{:S(2)}) async-start(bf16[32,6,16,512]{3,2,1,0:T(8,128)(2,1)} %get-tuple-element.57), calls=%async_computation.2 | async-start | bytes 6291456 | tf_op jit(solution)/shard_map/all_to_all | solution.py:1712
  586.4 75.9 %copy-start.11 = (s32[192]{0:T(256)S(1)}, s32[192]{0:T(256)}, u32[]{:S(2)}) copy-start(s32[192]{0:T(256)} %scatter_custom_fusion.slot_ref) | copy-start | bytes 2308
  586.5 91.2 %reduce-scatter.3.cloned.1.call-start = ((), (), s32[]{:S(2)}) async-start(), calls=%async_computation.4 | async-start | bytes 5242880 | tf_op jit(solution)/shard_map/reduce_scatter | solution.py:122
  673.0 3.9 copy-start.8
  673.0 3.9 copy-start.9
  673.0 3.9 copy-start.10
  673.0 76.9 %all-to-all-start.1 = ((bf16[32,6,16,512]{3,2,1,0:T(8,128)(2,1)}), bf16[32,6,16,512]{3,2,1,0:T(8,128)(2,1)}, u32[]{:S(2)}, u32[]{:S(2)}) async-start(bf16[32,6,16,512]{3,2,1,0:T(8,128)(2,1)} %precondition.1), calls=%async_computation.3 | async-start | bytes 6291456 | tf_op jit(solution)/shard_map/all_to_all | solution.py:1719
  677.6 3.3 copy-start.5
  680.9 8.7 %slice-start = ((s8[6291456]{0:T(1024)(128)(4,1)}), s8[4194304]{0:T(1024)(128)(4,1)S(1)}, s32[]{:S(2)}) async-start(s8[6291456]{0:T(1024)(128)(4,1)} %bitcast.51), calls=%async_computation.6 | async-start | bytes 8388608
  681.7 7.9 %slice-start.1 = ((s8[6291456]{0:T(1024)(128)(4,1)}), s8[2097152]{0:T(1024)(128)(4,1)S(1)}, s32[]{:S(2)}) async-start(s8[6291456]{0:T(1024)(128)(4,1)} %bitcast.51), calls=%async_computation.7 | async-start | bytes 4194304
  689.1 5.5 slice-start.2
  689.6 5.0 slice-start.3
  749.9 11.2 %copy-start.6 = (bf16[256,2048]{1,0:T(8,128)(2,1)S(1)}, bf16[256,2048]{1,0:T(8,128)(2,1)}, u32[]{:S(2)}) copy-start(bf16[256,2048]{1,0:T(8,128)(2,1)} %get-tuple-element.51) | copy-start | bytes 3145732
Sparse Core Ops, SparseCore 0:
  312.4 146.2 reduce-scatter.4
Sparse Core Ops, SparseCore 1:
  597.5 53.2 reduce-scatter.2
